TPU v7x, 512 devices: a whole 4x8x8 slice. The times are simulated.
512 devices in a mesh: dp: 64 (over x, y, core), tensor: 8 (over z).
Axes of the slice: x: 4, y: 8, z: 8, core: 2. Of those that a mesh axis runs over, the one named last changes fastest.
Arguments:
- queries: bfloat16 [8192, 4096], P('dp', 'tensor'), may hold values from -40 to 40
- keys: bfloat16 [106496, 1024], P(('dp', 'tensor')), may hold values from -40 to 40
- values: bfloat16 [106496, 1024], P(('dp', 'tensor')), may hold values from -6 to 6
- out_grad: bfloat16 [8192, 4096], P('dp', 'tensor'), may hold values from -6 to 6
- tile_counts: int32 [64], replicated, may hold values from 0 to 4, as said below
- text_sample: int32 [64], replicated, may hold values from 0 to 63, as said below
Outputs:
- query_grad: bfloat16 [8192, 4096], P('dp', 'tensor')
- key_grad: bfloat16 [106496, 1024], P(('dp', 'tensor'))
- value_grad: bfloat16 [106496, 1024], P(('dp', 'tensor'))
Inputs may be any that keep to these rules, and one draw needn't show every extreme that they name: `tile_counts`: the counts of each aligned group of 4 samples sum to 4. `text_sample`: each sample once; index i holds a sample of its own aligned group of 4 indices.
All inputs are finite; a program needn't handle non-finite values.
Results may differ from a plain program's by a relative error of at most 0.011.
Values may be sent and summed in bfloat16 or wider, within the bound.
No kernel may reach another device: no remote copies, remote signals or barrier semaphores. Data moves between devices by JAX's collectives and lax.ppermute only.
A program may use at most 64 MiB of HBM per device.

v0:
```python
import jax
import jax.numpy as jnp
from jax import lax
from jax.sharding import PartitionSpec as P

HEAD_DIM = 128
TILE_ROWS = 1601
TILE_PAD = 1664
TILE_DEV = 1
GROUP = 4


def from_behind(block, axis, distance):
    devices = range(lax.axis_size(axis))
    route = [(i - distance, i) for i in devices if i - distance in devices]
    return lax.ppermute(block, axis, route)


def gather_by_shifts(package, mover):
    position = lax.axis_index("dp") % GROUP
    received = [(0, package)]
    for offset in range(1 - GROUP, GROUP):
        if offset != 0:
            received.append((offset, mover(package, offset)))
    members = []
    for member in range(GROUP):
        picked = jnp.zeros_like(package)
        for offset, payload in received:
            picked = jnp.where(position - member == offset, payload, picked)
        members.append(picked)
    return jnp.stack(members)


def sum_by_shifts(shares, mover):
    position = lax.axis_index("dp") % GROUP
    running = lax.dynamic_index_in_dim(shares, position, 0, keepdims=False)
    for offset in range(1 - GROUP, GROUP):
        if offset != 0:
            target = position + offset
            in_group = (target >= 0) & (target < GROUP)
            outgoing = lax.dynamic_index_in_dim(
                shares, jnp.clip(target, 0, GROUP - 1), 0, keepdims=False
            )
            outgoing = jnp.where(in_group, outgoing, jnp.zeros_like(outgoing))
            running = running + mover(outgoing, offset)
    return running


def combine(first, second):
    top_value = jnp.maximum(first[0], second[0])
    left_scale = jnp.exp(first[0] - top_value)
    right_scale = jnp.exp(second[0] - top_value)
    return (
        top_value,
        first[1] * left_scale + second[1] * right_scale,
        first[2] * left_scale + second[2] * right_scale,
    )


def slot_scores(q_heads, g_heads, k_heads, v_heads):
    scores = jnp.einsum(
        "tkgd,rkd->kgtr", q_heads, k_heads, preferred_element_type=jnp.float32
    ) * HEAD_DIM ** (-0.5)
    live_rows = jnp.arange(k_heads.shape[0]) < TILE_ROWS
    scores = jnp.where(live_rows, scores, -1e30)
    grad_prod = jnp.einsum("tkgd,rkd->kgtr", g_heads, v_heads, preferred_element_type=jnp.float32)
    return (scores, grad_prod)


def on_device(queries, keys, values, out_grad, tile_counts, text_sample):
    softmax_scale = HEAD_DIM ** (-0.5)
    text_rows = queries.shape[0]
    width = queries.shape[1]
    kv_dev = keys.shape[1] // HEAD_DIM // lax.axis_size("tensor")
    per_kv = width // HEAD_DIM // kv_dev
    keys_here, values_here = (
        lax.all_to_all(keys, "tensor", split_axis=1, concat_axis=0, tiled=True),
        lax.all_to_all(values, "tensor", split_axis=1, concat_axis=0, tiled=True),
    )
    device = lax.axis_index("dp")
    position = device % GROUP
    package = jnp.stack([queries, out_grad])
    members = gather_by_shifts(package, lambda payload, offset: from_behind(payload, "dp", offset))
    tile_ends = jnp.cumsum(tile_counts)
    group_samples = lax.dynamic_slice_in_dim(text_sample, device - position, GROUP, 0)
    member_ids = jnp.arange(GROUP, dtype=jnp.int32)
    slot_index = device * TILE_DEV + 0
    sample_id = jnp.sum((tile_ends <= slot_index).astype(jnp.int32))
    member = jnp.sum(jnp.where(group_samples == sample_id, member_ids, 0))
    chosen = lax.dynamic_index_in_dim(members, member, 0, keepdims=False)
    q_heads = chosen[0].reshape(text_rows, kv_dev, per_kv, HEAD_DIM)
    g_heads = chosen[1].reshape(text_rows, kv_dev, per_kv, HEAD_DIM)
    k_heads = keys_here.reshape(TILE_PAD, kv_dev, HEAD_DIM)
    v_heads = values_here.reshape(TILE_PAD, kv_dev, HEAD_DIM)
    slot_members = [member]
    slot_inputs = [(q_heads, g_heads, k_heads, v_heads)]
    stat_shape = (GROUP, kv_dev, per_kv, text_rows)
    local_stats = (
        jnp.full(stat_shape, -1e30, jnp.float32),
        jnp.zeros(stat_shape, jnp.float32),
        jnp.zeros(stat_shape, jnp.float32),
    )
    for member, inputs in zip(slot_members, slot_inputs):
        scores, grad_prod = slot_scores(*inputs)
        maximum = jnp.max(scores, axis=-1)
        weights = jnp.exp(scores - maximum[..., None])
        totals = jnp.sum(weights, axis=-1)
        products = jnp.sum(weights * grad_prod, axis=-1)
        matched = (member_ids == member)[:, None, None, None]
        slot_stats = (
            jnp.where(matched, maximum[None], -1e30),
            jnp.where(matched, totals[None], 0.0),
            jnp.where(matched, products[None], 0.0),
        )
        local_stats = combine(local_stats, slot_stats)
    stat_block = jnp.stack(local_stats)
    gathered = gather_by_shifts(
        stat_block, lambda payload, offset: from_behind(payload, "dp", offset)
    )
    merged = (gathered[0, 0], gathered[0, 1], gathered[0, 2])
    for source in range(1, GROUP):
        merged = combine(merged, (gathered[source, 0], gathered[source, 1], gathered[source, 2]))
    safe_total = jnp.where(merged[1] > 0, merged[1], 1.0)
    log_total = merged[0] + jnp.log(safe_total)
    row_delta = merged[2] / safe_total
    contributions = jnp.zeros((GROUP, text_rows, width), jnp.float32)
    key_blocks = []
    value_blocks = []
    for member, inputs in zip(slot_members, slot_inputs):
        q_heads, g_heads, k_heads, v_heads = inputs
        scores, grad_prod = slot_scores(*inputs)
        member_log = lax.dynamic_index_in_dim(log_total, member, 0, keepdims=False)
        member_delta = lax.dynamic_index_in_dim(row_delta, member, 0, keepdims=False)
        probs = jnp.exp(scores - member_log[..., None])
        dscore = probs * (grad_prod - member_delta[..., None])
        probs_low = probs.astype(jnp.bfloat16)
        dscore_low = dscore.astype(jnp.bfloat16)
        value_part = jnp.einsum(
            "kgtr,tkgd->rkd", probs_low, g_heads, preferred_element_type=jnp.float32
        )
        key_part = (
            jnp.einsum("kgtr,tkgd->rkd", dscore_low, q_heads, preferred_element_type=jnp.float32)
            * softmax_scale
        )
        query_part = (
            jnp.einsum("kgtr,rkd->tkgd", dscore_low, k_heads, preferred_element_type=jnp.float32)
            * softmax_scale
        )
        matched = (member_ids == member)[:, None, None]
        contributions = jnp.where(matched, query_part.reshape(text_rows, width)[None], 0.0)
        key_blocks.append(key_part.reshape(TILE_PAD, kv_dev * HEAD_DIM).astype(jnp.bfloat16))
        value_blocks.append(value_part.reshape(TILE_PAD, kv_dev * HEAD_DIM).astype(jnp.bfloat16))
    key_local = key_blocks[0]
    value_local = value_blocks[0]
    key_grad, value_grad = (
        lax.all_to_all(key_local, "tensor", split_axis=0, concat_axis=1, tiled=True),
        lax.all_to_all(value_local, "tensor", split_axis=0, concat_axis=1, tiled=True),
    )
    own_grad = sum_by_shifts(
        contributions, lambda payload, offset: from_behind(payload, "dp", offset)
    )
    return (own_grad.astype(jnp.bfloat16), key_grad, value_grad)


def solution(mesh):
    return jax.shard_map(
        on_device,
        mesh=mesh,
        in_specs=(
            P("dp", "tensor"),
            P(("dp", "tensor"), None),
            P(("dp", "tensor"), None),
            P("dp", "tensor"),
            P(),
            P(),
        ),
        out_specs=(P("dp", "tensor"), P(("dp", "tensor"), None), P(("dp", "tensor"), None)),
        check_vma=False,
    )
```

profile of v0, /device:TPU:7, one launch (start us, length us, event | category | flops | bytes accessed | tf_op | source)
XLA Modules:
  0.0 153.2 jit_solution(12028790684278419533)
XLA Ops:
  0.6 0.0 copy-start
  0.6 1.1 copy.55
  1.7 1.0 copy.54
  2.8 4.8 %collective-permute-start = (bf16[2,128,512]{1,2,0:T(8,128)(2,1)S(1)}, bf16[2,128,512]{1,2,0:T(8,128)(2,1)S(1)}, u32[]{:S(2)}, u32[]{:S(2)}) collective-permute-start(bf16[2,128,512]{1,2,0:T(8,128)(2,1)S(1)} %pad_maximum_fusion), channel_id=1, source_target_pairs={{0,24},{8,32},{16,40},{24,48},{32,56},{40,64},{48,72},{56,80},{64,... | collective-permute-start | bytes 786440 | tf_op jit(solution)/shard_map/ppermute | solution.py:16
  7.6 3.2 %collective-permute-start.1 = (bf16[2,128,512]{1,2,0:T(8,128)(2,1)S(1)}, bf16[2,128,512]{1,2,0:T(8,128)(2,1)S(1)}, u32[]{:S(2)}, u32[]{:S(2)}) collective-permute-start(bf16[2,128,512]{1,2,0:T(8,128)(2,1)S(1)} %pad_maximum_fusion), channel_id=1, source_target_pairs={{0,16},{8,24},{16,32},{24,40},{32,48},{40,56},{48,64},{56,72},{64,... | collective-permute-start | bytes 786440 | tf_op jit(solution)/shard_map/ppermute | solution.py:16
  10.8 2.2 %collective-permute-start.2 = (bf16[2,128,512]{1,2,0:T(8,128)(2,1)S(1)}, bf16[2,128,512]{1,2,0:T(8,128)(2,1)S(1)}, u32[]{:S(2)}, u32[]{:S(2)}) collective-permute-start(bf16[2,128,512]{1,2,0:T(8,128)(2,1)S(1)} %pad_maximum_fusion), channel_id=1, source_target_pairs={{0,8},{8,16},{16,24},{24,32},{32,40},{40,48},{48,56},{56,64},{64,7... | collective-permute-start | bytes 786440 | tf_op jit(solution)/shard_map/ppermute | solution.py:16
  13.0 2.1 %collective-permute-start.3 = (bf16[2,128,512]{1,2,0:T(8,128)(2,1)S(1)}, bf16[2,128,512]{1,2,0:T(8,128)(2,1)S(1)}, u32[]{:S(2)}, u32[]{:S(2)}) collective-permute-start(bf16[2,128,512]{1,2,0:T(8,128)(2,1)S(1)} %pad_maximum_fusion), channel_id=1, source_target_pairs={{8,0},{16,8},{24,16},{32,24},{40,32},{48,40},{56,48},{64,56},{72,6... | collective-permute-start | bytes 786440 | tf_op jit(solution)/shard_map/ppermute | solution.py:16
  15.1 4.2 %collective-permute-start.4 = (bf16[2,128,512]{1,2,0:T(8,128)(2,1)S(1)}, bf16[2,128,512]{1,2,0:T(8,128)(2,1)S(1)}, u32[]{:S(2)}, u32[]{:S(2)}) collective-permute-start(bf16[2,128,512]{1,2,0:T(8,128)(2,1)S(1)} %pad_maximum_fusion), channel_id=1, source_target_pairs={{16,0},{24,8},{32,16},{40,24},{48,32},{56,40},{64,48},{72,56},{80,... | collective-permute-start | bytes 786440 | tf_op jit(solution)/shard_map/ppermute | solution.py:16
  19.3 0.8 copy_bitcast_fusion.3
  20.2 10.0 %all-to-all-start = ((bf16[208,8,128]{2,0,1:T(8,128)(2,1)}), bf16[208,8,128]{2,0,1:T(8,128)(2,1)S(1)}, u32[]{:S(2)}, u32[]{:S(2)}) async-start(bf16[208,8,128]{2,0,1:T(8,128)(2,1)} %copy_bitcast_fusion.3), calls=%async_computation | async-start | bytes 851968 | tf_op jit(solution)/shard_map/all_to_all | solution.py:77
  30.2 0.7 copy.53
  30.9 0.1 reduce-window.9
  31.0 0.6 convert_reduce_fusion
  31.7 2.0 %fusion.56 = s32[]{:T(128)} fusion(s32[64]{0:T(128)} %param.11, s32[]{:T(128)S(6)} %select_n.666, s32[]{:T(128)} %convert_reduce_fusion), kind=kLoop, calls=%fused_computation.129 | loop fusion | flops 11 | bytes 28 | tf_op jit(solution)/shard_map/reduce_sum | solution.py:89
  33.7 0.0 collective-permute-done
  33.7 3.0 %collective-permute-start.5 = (bf16[2,128,512]{1,2,0:T(8,128)(2,1)S(1)}, bf16[2,128,512]{1,2,0:T(8,128)(2,1)S(1)}, u32[]{:S(2)}, u32[]{:S(2)}) collective-permute-start(bf16[2,128,512]{1,2,0:T(8,128)(2,1)S(1)} %pad_maximum_fusion), channel_id=1, source_target_pairs={{24,0},{32,8},{40,16},{48,24},{56,32},{64,40},{72,48},{80,56},{88,... | collective-permute-start | bytes 786440 | tf_op jit(solution)/shard_map/ppermute | solution.py:16
  36.7 0.7 iota_compare_fusion.1
  39.4 1.8 %copy_bitcast_fusion.2 = bf16[208,8,128]{2,0,1:T(8,128)(2,1)} fusion(bf16[208,1024]{1,0:T(8,128)(2,1)} %param.8), kind=kLoop, calls=%fused_computation.29 | loop fusion | bytes 851968 | tf_op jit(solution)/shard_map/all_to_all | solution.py:78
  41.3 0.0 collective-permute-done.4
  41.3 6.3 %collective-permute-done.5 = bf16[2,128,512]{1,2,0:T(8,128)(2,1)S(1)} collective-permute-done((bf16[2,128,512]{1,2,0:T(8,128)(2,1)S(1)}, bf16[2,128,512]{1,2,0:T(8,128)(2,1)S(1)}, u32[]{:S(2)}, u32[]{:S(2)}) %collective-permute-start.5) | collective-permute-done | bytes 262176 | tf_op jit(solution)/shard_map/ppermute | solution.py:16
  47.6 0.1 select_bitcast_fusion.9
  47.7 0.8 select_bitcast_fusion.8
  48.5 0.8 select_bitcast_fusion.7
  49.3 6.1 %all-to-all-start.1 = ((bf16[208,8,128]{2,0,1:T(8,128)(2,1)}), bf16[208,8,128]{2,0,1:T(8,128)(2,1)S(1)}, u32[]{:S(2)}, u32[]{:S(2)}) async-start(bf16[208,8,128]{2,0,1:T(8,128)(2,1)} %copy_bitcast_fusion.2), calls=%async_computation.1 | async-start | bytes 851968 | tf_op jit(solution)/shard_map/all_to_all | solution.py:78
  55.4 0.1 select_bitcast_fusion.6
  55.5 1.2 fusion.17
  56.7 2.4 %fusion.59 = (f32[4,128]{1,0:T(4,128)S(1)}, f32[1,4,128,1664]{3,2,1,0:T(8,128)}) fusion(bf16[128,4,128]{0,2,1:T(8,128)(2,1)S(1)} %bitcast.315, bf16[1664,128,1]{1,0,2:T(8,128)(2,1)S(1)} %bitcast.310, pred[1664]{0:T(1024)(128)(4,1)S(1)} %iota_compare_fusion), kind=kOutput, calls=%fused_computation.132 | convolution fusion | flops 220659200 | bytes 3968640 | tf_op jit(solution)/shard_map/tkgd,rkd->kgtr/dot_general | solution.py:61
  59.1 10.4 %all-to-all-done.1 = bf16[208,8,128]{2,0,1:T(8,128)(2,1)S(1)} async-done(((bf16[208,8,128]{2,0,1:T(8,128)(2,1)}), bf16[208,8,128]{2,0,1:T(8,128)(2,1)S(1)}, u32[]{:S(2)}, u32[]{:S(2)}) %all-to-all-start.1) | async-done | bytes 426016 | tf_op jit(solution)/shard_map/all_to_all | solution.py:78
  69.6 4.7 %fusion.4 = (f32[4,128]{1,0:T(4,128)S(1)}, f32[4,128]{1,0:T(4,128)S(1)}, f32[128,4,1664]{2,0,1:T(8,128)}) fusion(f32[1,4,128,1664]{3,2,1,0:T(8,128)} %get-tuple-element.27, f32[4,128]{1,0:T(4,128)S(1)} %get-tuple-element.26, bf16[128,4,128]{0,2,1:T(8,128)(2,1)S(1)} %bitcast.313, bf16[1664,128,1]{1,0,2:T(8,128)(2,1)S(1)} %bitcast.312), kind=kOutput, calls=%fused_computation.9 | convolution fusion | flops 221510656 | bytes 7378944 | tf_op jit(solution)/shard_map/tkgd,rkd->kgtr/dot_general | solution.py:66
  74.2 0.1 select_maximum_fusion.1
  74.4 4.0 %collective-permute-start.6 = (f32[3,4,1,4,128]{4,3,1,0,2:T(4,128)S(1)}, f32[3,4,1,4,128]{4,3,1,0,2:T(4,128)S(1)}, u32[]{:S(2)}, u32[]{:S(2)}) collective-permute-start(f32[3,4,1,4,128]{4,3,1,0,2:T(4,128)S(1)} %pad_maximum_fusion.1), channel_id=1, source_target_pairs={{0,24},{8,32},{16,40},{24,48},{32,56},{40,64},{48,72},{56,80},{64,... | collective-permute-start | bytes 73736 | tf_op jit(solution)/shard_map/ppermute | solution.py:16
  78.4 5.5 %collective-permute-start.7 = (f32[3,4,1,4,128]{4,3,1,0,2:T(4,128)S(1)}, f32[3,4,1,4,128]{4,3,1,0,2:T(4,128)S(1)}, u32[]{:S(2)}, u32[]{:S(2)}) collective-permute-start(f32[3,4,1,4,128]{4,3,1,0,2:T(4,128)S(1)} %pad_maximum_fusion.1), channel_id=1, source_target_pairs={{0,16},{8,24},{16,32},{24,40},{32,48},{40,56},{48,64},{56,72},{64,... | collective-permute-start | bytes 73736 | tf_op jit(solution)/shard_map/ppermute | solution.py:16
  83.9 1.9 %collective-permute-start.8 = (f32[3,4,1,4,128]{4,3,1,0,2:T(4,128)S(1)}, f32[3,4,1,4,128]{4,3,1,0,2:T(4,128)S(1)}, u32[]{:S(2)}, u32[]{:S(2)}) collective-permute-start(f32[3,4,1,4,128]{4,3,1,0,2:T(4,128)S(1)} %pad_maximum_fusion.1), channel_id=1, source_target_pairs={{0,8},{8,16},{16,24},{24,32},{32,40},{40,48},{48,56},{56,64},{64,7... | collective-permute-start | bytes 73736 | tf_op jit(solution)/shard_map/ppermute | solution.py:16
  85.8 2.4 %collective-permute-start.9 = (f32[3,4,1,4,128]{4,3,1,0,2:T(4,128)S(1)}, f32[3,4,1,4,128]{4,3,1,0,2:T(4,128)S(1)}, u32[]{:S(2)}, u32[]{:S(2)}) collective-permute-start(f32[3,4,1,4,128]{4,3,1,0,2:T(4,128)S(1)} %pad_maximum_fusion.1), channel_id=1, source_target_pairs={{8,0},{16,8},{24,16},{32,24},{40,32},{48,40},{56,48},{64,56},{72,6... | collective-permute-start | bytes 73736 | tf_op jit(solution)/shard_map/ppermute | solution.py:16
  88.2 3.3 %collective-permute-start.10 = (f32[3,4,1,4,128]{4,3,1,0,2:T(4,128)S(1)}, f32[3,4,1,4,128]{4,3,1,0,2:T(4,128)S(1)}, u32[]{:S(2)}, u32[]{:S(2)}) collective-permute-start(f32[3,4,1,4,128]{4,3,1,0,2:T(4,128)S(1)} %pad_maximum_fusion.1), channel_id=1, source_target_pairs={{16,0},{24,8},{32,16},{40,24},{48,32},{56,40},{64,48},{72,56},{80,... | collective-permute-start | bytes 73736 | tf_op jit(solution)/shard_map/ppermute | solution.py:16
  91.5 0.0 collective-permute-done.6
  91.5 3.9 %collective-permute-start.11 = (f32[3,4,1,4,128]{4,3,1,0,2:T(4,128)S(1)}, f32[3,4,1,4,128]{4,3,1,0,2:T(4,128)S(1)}, u32[]{:S(2)}, u32[]{:S(2)}) collective-permute-start(f32[3,4,1,4,128]{4,3,1,0,2:T(4,128)S(1)} %pad_maximum_fusion.1), channel_id=1, source_target_pairs={{24,0},{32,8},{40,16},{48,24},{56,32},{64,40},{72,48},{80,56},{88,... | collective-permute-start | bytes 73736 | tf_op jit(solution)/shard_map/ppermute | solution.py:16
  95.4 0.1 fusion.25
  95.5 0.0 collective-permute-done.8
  95.5 0.0 collective-permute-done.9
  95.5 2.3 %collective-permute-done.11 = f32[3,4,1,4,128]{4,3,1,0,2:T(4,128)S(1)} collective-permute-done((f32[3,4,1,4,128]{4,3,1,0,2:T(4,128)S(1)}, f32[3,4,1,4,128]{4,3,1,0,2:T(4,128)S(1)}, u32[]{:S(2)}, u32[]{:S(2)}) %collective-permute-start.11) | collective-permute-done | bytes 24608 | tf_op jit(solution)/shard_map/ppermute | solution.py:16
  98.0 3.7 %fusion.13 = bf16[4,128,1664]{2,1,0:T(8,128)(2,1)S(1)} fusion(f32[128,4,1664]{2,0,1:T(8,128)} %get-tuple-element.28, f32[1,4,128,1664]{3,2,1,0:T(8,128)} %get-tuple-element.27, f32[4,128]{1,0:T(4,128)S(1)} %get-tuple-element.19, f32[4,128]{1,0:T(4,128)S(1)} %get-tuple-element.18), kind=kLoop, calls=%fused_computation.19 | loop fusion | flops 3407872 | bytes 8523776 | tf_op jit(solution)/shard_map/reshape.32
  101.8 0.7 convolution_multiply_fusion
  102.5 0.4 fusion.10
  102.9 0.1 copy.73
  103.1 1.0 copy.74
  104.0 3.5 %all-to-all-start.2 = ((bf16[8,208,128]{2,1,0:T(8,128)(2,1)}), bf16[8,208,128]{2,1,0:T(8,128)(2,1)S(1)}, u32[]{:S(2)}, u32[]{:S(2)}) async-start(bf16[8,208,128]{2,1,0:T(8,128)(2,1)} %bitcast.73), calls=%async_computation.2 | async-start | bytes 851968 | tf_op jit(solution)/shard_map/all_to_all | solution.py:156
  107.5 0.2 broadcast_select_fusion
  107.7 1.1 select_bitcast_fusion.5
  108.8 2.3 %collective-permute-start.17 = (f32[128,512]{1,0:T(8,128)S(1)}, f32[128,512]{1,0:T(8,128)S(1)}, u32[]{:S(2)}, u32[]{:S(2)}) collective-permute-start(f32[128,512]{1,0:T(8,128)S(1)} %get-tuple-element.11), channel_id=1, source_target_pairs={{0,24},{8,32},{16,40},{24,48},{32,56},{40,64},{48,72},{56,80},{64,... | collective-permute-start | bytes 786440 | tf_op jit(solution)/shard_map/ppermute | solution.py:16
  111.1 3.8 %collective-permute-start.16 = (f32[128,512]{1,0:T(8,128)}, f32[128,512]{1,0:T(8,128)S(1)}, u32[]{:S(2)}, u32[]{:S(2)}) collective-permute-start(f32[128,512]{1,0:T(8,128)} %get-tuple-element.12), channel_id=1, source_target_pairs={{0,16},{8,24},{16,32},{24,40},{32,48},{40,56},{48,64},{56,72},{64,... | collective-permute-start | bytes 786440 | tf_op jit(solution)/shard_map/ppermute | solution.py:16
  114.9 1.9 %collective-permute-start.15 = (f32[128,512]{1,0:T(8,128)}, f32[128,512]{1,0:T(8,128)S(1)}, u32[]{:S(2)}, u32[]{:S(2)}) collective-permute-start(f32[128,512]{1,0:T(8,128)} %get-tuple-element.13), channel_id=1, source_target_pairs={{0,8},{8,16},{16,24},{24,32},{32,40},{40,48},{48,56},{56,64},{64,7... | collective-permute-start | bytes 786440 | tf_op jit(solution)/shard_map/ppermute | solution.py:16
  116.9 2.4 %collective-permute-start.14 = (f32[128,512]{1,0:T(8,128)}, f32[128,512]{1,0:T(8,128)S(1)}, u32[]{:S(2)}, u32[]{:S(2)}) collective-permute-start(f32[128,512]{1,0:T(8,128)} %get-tuple-element.14), channel_id=1, source_target_pairs={{8,0},{16,8},{24,16},{32,24},{40,32},{48,40},{56,48},{64,56},{72,6... | collective-permute-start | bytes 786440 | tf_op jit(solution)/shard_map/ppermute | solution.py:16
  119.3 4.8 %collective-permute-start.13 = (f32[128,512]{1,0:T(8,128)}, f32[128,512]{1,0:T(8,128)}, u32[]{:S(2)}, u32[]{:S(2)}) collective-permute-start(f32[128,512]{1,0:T(8,128)} %get-tuple-element.15), channel_id=1, source_target_pairs={{16,0},{24,8},{32,16},{40,24},{48,32},{56,40},{64,48},{72,56},{80,... | collective-permute-start | bytes 786440 | tf_op jit(solution)/shard_map/ppermute | solution.py:16
  124.1 0.0 collective-permute-done.17
  124.2 3.9 %collective-permute-start.12 = (f32[128,512]{1,0:T(8,128)}, f32[128,512]{1,0:T(8,128)}, u32[]{:S(2)}, u32[]{:S(2)}) collective-permute-start(f32[128,512]{1,0:T(8,128)} %get-tuple-element.10), channel_id=1, source_target_pairs={{24,0},{32,8},{40,16},{48,24},{56,32},{64,40},{72,48},{80,56},{88,... | collective-permute-start | bytes 786440 | tf_op jit(solution)/shard_map/ppermute | solution.py:16
  128.1 0.8 fusion.9
  128.9 1.0 copy.76
  129.9 6.6 %all-to-all-start.3 = ((bf16[8,208,128]{2,1,0:T(8,128)(2,1)}), bf16[8,208,128]{2,1,0:T(8,128)(2,1)S(1)}, u32[]{:S(2)}, u32[]{:S(2)}) async-start(bf16[8,208,128]{2,1,0:T(8,128)(2,1)} %bitcast.79), calls=%async_computation.3 | async-start | bytes 851968 | tf_op jit(solution)/shard_map/all_to_all | solution.py:157
  136.5 2.7 %collective-permute-done.12 = f32[128,512]{1,0:T(8,128)} collective-permute-done((f32[128,512]{1,0:T(8,128)}, f32[128,512]{1,0:T(8,128)}, u32[]{:S(2)}, u32[]{:S(2)}) %collective-permute-start.12) | collective-permute-done | bytes 262176 | tf_op jit(solution)/shard_map/ppermute | solution.py:16
  139.2 1.8 %fusion.23 = bf16[128,512]{1,0:T(8,128)(2,1)} fusion(f32[128,512]{1,0:T(8,128)S(1)} %collective-permute-done.17, f32[128,512]{1,0:T(8,128)S(1)} %collective-permute-done.16, f32[128,512]{1,0:T(8,128)S(1)} %collective-permute-done.15, f32[128,512]{1,0:T(8,128)S(1)} %collective-permute-done.14, f32[128,512]{1,0:T(8,128)} %collective-permute-done.13, ...), kind=kLoop, calls=%fused_computation.41 | loop fusion | flops 458752 | bytes 1966084 | tf_op jit(solution)/shard_map/convert_element_type | solution.py:162
  141.0 0.8 copy_bitcast_fusion.1
  141.8 10.6 %all-to-all-done.3 = bf16[8,208,128]{2,1,0:T(8,128)(2,1)S(1)} async-done(((bf16[8,208,128]{2,1,0:T(8,128)(2,1)}), bf16[8,208,128]{2,1,0:T(8,128)(2,1)S(1)}, u32[]{:S(2)}, u32[]{:S(2)}) %all-to-all-start.3) | async-done | bytes 426016 | tf_op jit(solution)/shard_map/all_to_all | solution.py:157
  152.4 0.8 copy_bitcast_fusion
  (26 shorter events, 0.3 us)
Async XLA Ops:
  0.6 18.7 %copy-start = (bf16[208,1024]{1,0:T(8,128)(2,1)S(1)}, bf16[208,1024]{1,0:T(8,128)(2,1)}, u32[]{:S(2)}) copy-start(bf16[208,1024]{1,0:T(8,128)(2,1)} %param.7) | copy-start | bytes 1277956
  2.8 30.9 %collective-permute-start = (bf16[2,128,512]{1,2,0:T(8,128)(2,1)S(1)}, bf16[2,128,512]{1,2,0:T(8,128)(2,1)S(1)}, u32[]{:S(2)}, u32[]{:S(2)}) collective-permute-start(bf16[2,128,512]{1,2,0:T(8,128)(2,1)S(1)} %pad_maximum_fusion), channel_id=1, source_target_pairs={{0,24},{8,32},{16,40},{24,48},{32,56},{40,64},{48,72},{56,80},{64,... | collective-permute-start | bytes 786440 | tf_op jit(solution)/shard_map/ppermute | solution.py:16
  7.6 33.7 %collective-permute-start.1 = (bf16[2,128,512]{1,2,0:T(8,128)(2,1)S(1)}, bf16[2,128,512]{1,2,0:T(8,128)(2,1)S(1)}, u32[]{:S(2)}, u32[]{:S(2)}) collective-permute-start(bf16[2,128,512]{1,2,0:T(8,128)(2,1)S(1)} %pad_maximum_fusion), channel_id=1, source_target_pairs={{0,16},{8,24},{16,32},{24,40},{32,48},{40,56},{48,64},{56,72},{64,... | collective-permute-start | bytes 786440 | tf_op jit(solution)/shard_map/ppermute | solution.py:16
  10.8 30.5 %collective-permute-start.2 = (bf16[2,128,512]{1,2,0:T(8,128)(2,1)S(1)}, bf16[2,128,512]{1,2,0:T(8,128)(2,1)S(1)}, u32[]{:S(2)}, u32[]{:S(2)}) collective-permute-start(bf16[2,128,512]{1,2,0:T(8,128)(2,1)S(1)} %pad_maximum_fusion), channel_id=1, source_target_pairs={{0,8},{8,16},{16,24},{24,32},{32,40},{40,48},{48,56},{56,64},{64,7... | collective-permute-start | bytes 786440 | tf_op jit(solution)/shard_map/ppermute | solution.py:16
  13.0 28.3 %collective-permute-start.3 = (bf16[2,128,512]{1,2,0:T(8,128)(2,1)S(1)}, bf16[2,128,512]{1,2,0:T(8,128)(2,1)S(1)}, u32[]{:S(2)}, u32[]{:S(2)}) collective-permute-start(bf16[2,128,512]{1,2,0:T(8,128)(2,1)S(1)} %pad_maximum_fusion), channel_id=1, source_target_pairs={{8,0},{16,8},{24,16},{32,24},{40,32},{48,40},{56,48},{64,56},{72,6... | collective-permute-start | bytes 786440 | tf_op jit(solution)/shard_map/ppermute | solution.py:16
  15.1 26.1 %collective-permute-start.4 = (bf16[2,128,512]{1,2,0:T(8,128)(2,1)S(1)}, bf16[2,128,512]{1,2,0:T(8,128)(2,1)S(1)}, u32[]{:S(2)}, u32[]{:S(2)}) collective-permute-start(bf16[2,128,512]{1,2,0:T(8,128)(2,1)S(1)} %pad_maximum_fusion), channel_id=1, source_target_pairs={{16,0},{24,8},{32,16},{40,24},{48,32},{56,40},{64,48},{72,56},{80,... | collective-permute-start | bytes 786440 | tf_op jit(solution)/shard_map/ppermute | solution.py:16
  20.2 29.1 %all-to-all-start = ((bf16[208,8,128]{2,0,1:T(8,128)(2,1)}), bf16[208,8,128]{2,0,1:T(8,128)(2,1)S(1)}, u32[]{:S(2)}, u32[]{:S(2)}) async-start(bf16[208,8,128]{2,0,1:T(8,128)(2,1)} %copy_bitcast_fusion.3), calls=%async_computation | async-start | bytes 851968 | tf_op jit(solution)/shard_map/all_to_all | solution.py:77
  33.7 13.9 %collective-permute-start.5 = (bf16[2,128,512]{1,2,0:T(8,128)(2,1)S(1)}, bf16[2,128,512]{1,2,0:T(8,128)(2,1)S(1)}, u32[]{:S(2)}, u32[]{:S(2)}) collective-permute-start(bf16[2,128,512]{1,2,0:T(8,128)(2,1)S(1)} %pad_maximum_fusion), channel_id=1, source_target_pairs={{24,0},{32,8},{40,16},{48,24},{56,32},{64,40},{72,48},{80,56},{88,... | collective-permute-start | bytes 786440 | tf_op jit(solution)/shard_map/ppermute | solution.py:16
  49.3 20.3 %all-to-all-start.1 = ((bf16[208,8,128]{2,0,1:T(8,128)(2,1)}), bf16[208,8,128]{2,0,1:T(8,128)(2,1)S(1)}, u32[]{:S(2)}, u32[]{:S(2)}) async-start(bf16[208,8,128]{2,0,1:T(8,128)(2,1)} %copy_bitcast_fusion.2), calls=%async_computation.1 | async-start | bytes 851968 | tf_op jit(solution)/shard_map/all_to_all | solution.py:78
  74.4 17.1 %collective-permute-start.6 = (f32[3,4,1,4,128]{4,3,1,0,2:T(4,128)S(1)}, f32[3,4,1,4,128]{4,3,1,0,2:T(4,128)S(1)}, u32[]{:S(2)}, u32[]{:S(2)}) collective-permute-start(f32[3,4,1,4,128]{4,3,1,0,2:T(4,128)S(1)} %pad_maximum_fusion.1), channel_id=1, source_target_pairs={{0,24},{8,32},{16,40},{24,48},{32,56},{40,64},{48,72},{56,80},{64,... | collective-permute-start | bytes 73736 | tf_op jit(solution)/shard_map/ppermute | solution.py:16
  78.4 17.1 %collective-permute-start.7 = (f32[3,4,1,4,128]{4,3,1,0,2:T(4,128)S(1)}, f32[3,4,1,4,128]{4,3,1,0,2:T(4,128)S(1)}, u32[]{:S(2)}, u32[]{:S(2)}) collective-permute-start(f32[3,4,1,4,128]{4,3,1,0,2:T(4,128)S(1)} %pad_maximum_fusion.1), channel_id=1, source_target_pairs={{0,16},{8,24},{16,32},{24,40},{32,48},{40,56},{48,64},{56,72},{64,... | collective-permute-start | bytes 73736 | tf_op jit(solution)/shard_map/ppermute | solution.py:16
  83.9 11.6 %collective-permute-start.8 = (f32[3,4,1,4,128]{4,3,1,0,2:T(4,128)S(1)}, f32[3,4,1,4,128]{4,3,1,0,2:T(4,128)S(1)}, u32[]{:S(2)}, u32[]{:S(2)}) collective-permute-start(f32[3,4,1,4,128]{4,3,1,0,2:T(4,128)S(1)} %pad_maximum_fusion.1), channel_id=1, source_target_pairs={{0,8},{8,16},{16,24},{24,32},{32,40},{40,48},{48,56},{56,64},{64,7... | collective-permute-start | bytes 73736 | tf_op jit(solution)/shard_map/ppermute | solution.py:16
  85.8 9.7 %collective-permute-start.9 = (f32[3,4,1,4,128]{4,3,1,0,2:T(4,128)S(1)}, f32[3,4,1,4,128]{4,3,1,0,2:T(4,128)S(1)}, u32[]{:S(2)}, u32[]{:S(2)}) collective-permute-start(f32[3,4,1,4,128]{4,3,1,0,2:T(4,128)S(1)} %pad_maximum_fusion.1), channel_id=1, source_target_pairs={{8,0},{16,8},{24,16},{32,24},{40,32},{48,40},{56,48},{64,56},{72,6... | collective-permute-start | bytes 73736 | tf_op jit(solution)/shard_map/ppermute | solution.py:16
  88.2 7.3 %collective-permute-start.10 = (f32[3,4,1,4,128]{4,3,1,0,2:T(4,128)S(1)}, f32[3,4,1,4,128]{4,3,1,0,2:T(4,128)S(1)}, u32[]{:S(2)}, u32[]{:S(2)}) collective-permute-start(f32[3,4,1,4,128]{4,3,1,0,2:T(4,128)S(1)} %pad_maximum_fusion.1), channel_id=1, source_target_pairs={{16,0},{24,8},{32,16},{40,24},{48,32},{56,40},{64,48},{72,56},{80,... | collective-permute-start | bytes 73736 | tf_op jit(solution)/shard_map/ppermute | solution.py:16
  91.5 6.3 %collective-permute-start.11 = (f32[3,4,1,4,128]{4,3,1,0,2:T(4,128)S(1)}, f32[3,4,1,4,128]{4,3,1,0,2:T(4,128)S(1)}, u32[]{:S(2)}, u32[]{:S(2)}) collective-permute-start(f32[3,4,1,4,128]{4,3,1,0,2:T(4,128)S(1)} %pad_maximum_fusion.1), channel_id=1, source_target_pairs={{24,0},{32,8},{40,16},{48,24},{56,32},{64,40},{72,48},{80,56},{88,... | collective-permute-start | bytes 73736 | tf_op jit(solution)/shard_map/ppermute | solution.py:16
  104.0 25.8 %all-to-all-start.2 = ((bf16[8,208,128]{2,1,0:T(8,128)(2,1)}), bf16[8,208,128]{2,1,0:T(8,128)(2,1)S(1)}, u32[]{:S(2)}, u32[]{:S(2)}) async-start(bf16[8,208,128]{2,1,0:T(8,128)(2,1)} %bitcast.73), calls=%async_computation.2 | async-start | bytes 851968 | tf_op jit(solution)/shard_map/all_to_all | solution.py:156
  107.5 20.6 %copy-start.1 = (f32[1,4,128,1664]{3,2,1,0:T(8,128)S(1)}, f32[1,4,128,1664]{3,2,1,0:T(8,128)}, u32[]{:S(2)}) copy-start(f32[1,4,128,1664]{3,2,1,0:T(8,128)} %get-tuple-element.27) | copy-start | bytes 10223620
  108.8 15.4 %collective-permute-start.17 = (f32[128,512]{1,0:T(8,128)S(1)}, f32[128,512]{1,0:T(8,128)S(1)}, u32[]{:S(2)}, u32[]{:S(2)}) collective-permute-start(f32[128,512]{1,0:T(8,128)S(1)} %get-tuple-element.11), channel_id=1, source_target_pairs={{0,24},{8,32},{16,40},{24,48},{32,56},{40,64},{48,72},{56,80},{64,... | collective-permute-start | bytes 786440 | tf_op jit(solution)/shard_map/ppermute | solution.py:16
  111.1 25.4 %collective-permute-start.16 = (f32[128,512]{1,0:T(8,128)}, f32[128,512]{1,0:T(8,128)S(1)}, u32[]{:S(2)}, u32[]{:S(2)}) collective-permute-start(f32[128,512]{1,0:T(8,128)} %get-tuple-element.12), channel_id=1, source_target_pairs={{0,16},{8,24},{16,32},{24,40},{32,48},{40,56},{48,64},{56,72},{64,... | collective-permute-start | bytes 786440 | tf_op jit(solution)/shard_map/ppermute | solution.py:16
  114.9 21.6 %collective-permute-start.15 = (f32[128,512]{1,0:T(8,128)}, f32[128,512]{1,0:T(8,128)S(1)}, u32[]{:S(2)}, u32[]{:S(2)}) collective-permute-start(f32[128,512]{1,0:T(8,128)} %get-tuple-element.13), channel_id=1, source_target_pairs={{0,8},{8,16},{16,24},{24,32},{32,40},{40,48},{48,56},{56,64},{64,7... | collective-permute-start | bytes 786440 | tf_op jit(solution)/shard_map/ppermute | solution.py:16
  116.9 19.6 %collective-permute-start.14 = (f32[128,512]{1,0:T(8,128)}, f32[128,512]{1,0:T(8,128)S(1)}, u32[]{:S(2)}, u32[]{:S(2)}) collective-permute-start(f32[128,512]{1,0:T(8,128)} %get-tuple-element.14), channel_id=1, source_target_pairs={{8,0},{16,8},{24,16},{32,24},{40,32},{48,40},{56,48},{64,56},{72,6... | collective-permute-start | bytes 786440 | tf_op jit(solution)/shard_map/ppermute | solution.py:16
  119.3 17.2 %collective-permute-start.13 = (f32[128,512]{1,0:T(8,128)}, f32[128,512]{1,0:T(8,128)}, u32[]{:S(2)}, u32[]{:S(2)}) collective-permute-start(f32[128,512]{1,0:T(8,128)} %get-tuple-element.15), channel_id=1, source_target_pairs={{16,0},{24,8},{32,16},{40,24},{48,32},{56,40},{64,48},{72,56},{80,... | collective-permute-start | bytes 786440 | tf_op jit(solution)/shard_map/ppermute | solution.py:16
  124.2 15.0 %collective-permute-start.12 = (f32[128,512]{1,0:T(8,128)}, f32[128,512]{1,0:T(8,128)}, u32[]{:S(2)}, u32[]{:S(2)}) collective-permute-start(f32[128,512]{1,0:T(8,128)} %get-tuple-element.10), channel_id=1, source_target_pairs={{24,0},{32,8},{40,16},{48,24},{56,32},{64,40},{72,48},{80,56},{88,... | collective-permute-start | bytes 786440 | tf_op jit(solution)/shard_map/ppermute | solution.py:16
  129.9 22.6 %all-to-all-start.3 = ((bf16[8,208,128]{2,1,0:T(8,128)(2,1)}), bf16[8,208,128]{2,1,0:T(8,128)(2,1)S(1)}, u32[]{:S(2)}, u32[]{:S(2)}) async-start(bf16[8,208,128]{2,1,0:T(8,128)(2,1)} %bitcast.79), calls=%async_computation.3 | async-start | bytes 851968 | tf_op jit(solution)/shard_map/all_to_all | solution.py:157
where the time goes:
time: 154 us; the launch traced here: 153 us
  starting transfers between devices  85.9 us (56%)
  waiting for transfers between devices  32.4 us (21%)
  other arithmetic  13.6 us (9%)
  local copies, waits for them, and re-layouts  9.24 us (6%)
  matrix products  9.08 us (6%)
  between operations  3.11 us (2%)
    ppermute x18, starting transfers between devices, from_behind(): return lax.ppermute(block, axis, route)  59.6 us
    ppermute x18, waiting for transfers between devices, from_behind(): return lax.ppermute(block, axis, route)  11.3 us
    all_to_all x1, waiting for transfers between devices, on_device(): lax.all_to_all(value_local, 'tensor', split_axis=0, concat_axis=1, tiled=...  10.6 us
    all_to_all x1, waiting for transfers between devices, on_device(): lax.all_to_all(values, 'tensor', split_axis=1, concat_axis=0, tiled=True)  10.4 us
    all_to_all x1, starting transfers between devices, on_device(): lax.all_to_all(keys, 'tensor', split_axis=1, concat_axis=0, tiled=True)  10 us
    all_to_all x1, starting transfers between devices, on_device(): lax.all_to_all(value_local, 'tensor', split_axis=0, concat_axis=1, tiled=...  6.6 us
    all_to_all x1, starting transfers between devices, on_device(): lax.all_to_all(values, 'tensor', split_axis=1, concat_axis=0, tiled=True)  6.14 us
    dot_general x1, matrix products, slot_scores(): jnp.einsum('tkgd,rkd->kgtr', g_heads, v_heads, preferred_element_type=jnp...  4.69 us
  transfers between devices with their start and end apart: 22, of which 5 were waited for; matrix products, arithmetic and copies ran while one was open for 12% of the time, Pallas kernels for 0%

commit v1 on v0

v1 whole, which is shorter than its diff:
```python
import functools

import jax
import jax.numpy as jnp
from jax import lax
from jax.experimental import pallas as pl
from jax.experimental.pallas import tpu as pltpu
from jax.sharding import PartitionSpec as P

HEAD_DIM = 128
TILE_ROWS = 1601
GROUP = 4
SCALE = HEAD_DIM ** -0.5
LOG2E = 1.4426950408889634
SCALE2 = SCALE * LOG2E


def owners(dp, counts, text):
    first = (dp // GROUP) * GROUP
    end0 = counts[first]
    end1 = end0 + counts[first + 1]
    end2 = end1 + counts[first + 2]
    found = []
    for slot in range(GROUP):
        sample = first
        for end in (end0, end1, end2):
            sample = sample + jnp.where(end <= slot, 1, 0)
        owner = jnp.int32(0)
        for member in range(1, GROUP):
            owner = owner + jnp.where(text[first + member] == sample, member, 0)
        found.append(owner)
    return found, dp - first


def pick(options, position):
    chosen = options[0]
    for index in range(1, GROUP):
        chosen = jnp.where(position == index, options[index], chosen)
    return chosen


def head_rows(block):
    heads = block.shape[1] // HEAD_DIM
    return jnp.concatenate([block[:, h * HEAD_DIM:(h + 1) * HEAD_DIM] for h in range(heads)], axis=0)


def scores_of(kv_ref, part, q_rows):
    rows = kv_ref.shape[2]
    scores = lax.dot_general(
        kv_ref[part, 0], q_rows, (((1,), (1,)), ((), ())), preferred_element_type=jnp.float32
    ) * SCALE2
    if (part + 1) * rows > TILE_ROWS:
        row = lax.broadcasted_iota(jnp.int32, scores.shape, 0) + part * rows
        scores = jnp.where(row < TILE_ROWS, scores, -1e30)
    return scores


def grad_of(kv_ref, part, g_rows):
    return lax.dot_general(
        kv_ref[part, 1], g_rows, (((1,), (1,)), ((), ())), preferred_element_type=jnp.float32
    )


def stats_kernel(dp_ref, counts_ref, text_ref, q_ref, g_ref, kv_ref, stat_ref, score_ref):
    found, position = owners(dp_ref[0], counts_ref, text_ref)
    mine = pick(found, position)
    q_rows = head_rows(q_ref[mine])
    g_rows = head_rows(g_ref[mine])
    parts, rows = kv_ref.shape[0], kv_ref.shape[2]
    top = None
    for part in range(parts):
        scores = scores_of(kv_ref, part, q_rows)
        score_ref[pl.ds(part * rows, rows), :] = scores
        part_top = jnp.max(scores, axis=0, keepdims=True)
        top = part_top if top is None else jnp.maximum(top, part_top)
    total = jnp.zeros_like(top)
    product = jnp.zeros_like(top)
    for part in range(parts):
        weights = jnp.exp2(score_ref[pl.ds(part * rows, rows), :] - top)
        total = total + jnp.sum(weights, axis=0, keepdims=True)
        product = product + jnp.sum(weights * grad_of(kv_ref, part, g_rows), axis=0, keepdims=True)
    stat_ref[...] = jnp.concatenate([top, total, product, jnp.zeros((5, top.shape[1]), jnp.float32)], axis=0)


def grads_kernel(dp_ref, counts_ref, text_ref, stat_ref, q_ref, g_ref, kv_ref, out_ref, dq_ref):
    found, position = owners(dp_ref[0], counts_ref, text_ref)
    mine = pick(found, position)
    q_rows = head_rows(q_ref[mine])
    g_rows = head_rows(g_ref[mine])
    stats = []
    top = None
    for slot in range(GROUP):
        same = found[slot] == mine
        block = stat_ref[slot]
        slot_top = jnp.where(same, block[0:1], -1e30)
        stats.append((same, slot_top, block[1:2], block[2:3]))
        top = slot_top if top is None else jnp.maximum(top, slot_top)
    total = jnp.zeros_like(top)
    product = jnp.zeros_like(top)
    for same, slot_top, slot_total, slot_product in stats:
        weight = jnp.where(same, jnp.exp2(slot_top - top), 0.0)
        total = total + weight * slot_total
        product = product + weight * slot_product
    log_total = top + jnp.log2(total)
    delta = product / total
    parts = kv_ref.shape[0]
    dq = None
    for part in range(parts):
        probs = jnp.exp2(scores_of(kv_ref, part, q_rows) - log_total)
        dscore = probs * (grad_of(kv_ref, part, g_rows) - delta)
        probs = probs.astype(jnp.bfloat16)
        dscore = dscore.astype(jnp.bfloat16)
        value_part = jnp.dot(probs, g_rows, preferred_element_type=jnp.float32)
        key_part = jnp.dot(dscore, q_rows, preferred_element_type=jnp.float32) * SCALE
        out_ref[part, 0] = key_part.astype(jnp.bfloat16)
        out_ref[part, 1] = value_part.astype(jnp.bfloat16)
        query_part = lax.dot_general(
            kv_ref[part, 0], dscore, (((0,), (0,)), ((), ())), preferred_element_type=jnp.float32
        )
        dq = query_part if dq is None else dq + query_part
    for head in range(dq.shape[1] // HEAD_DIM):
        cols = slice(head * HEAD_DIM, (head + 1) * HEAD_DIM)
        dq_ref[:, cols] = (dq[:, cols].T * SCALE).astype(jnp.bfloat16)


def query_kernel(dp_ref, counts_ref, text_ref, parts_ref, out_ref):
    found, position = owners(dp_ref[0], counts_ref, text_ref)
    total = jnp.zeros(out_ref.shape, jnp.float32)
    for slot in range(GROUP):
        total = total + jnp.where(found[slot] == position, parts_ref[slot].astype(jnp.float32), 0.0)
    out_ref[...] = total.astype(jnp.bfloat16)


SMEM = pl.BlockSpec(memory_space=pltpu.SMEM)
VMEM = pl.BlockSpec(memory_space=pltpu.VMEM)


def call(kernel, out_shape, scalars, arrays, scratch=(), flops=0, exps=0):
    outs = out_shape if isinstance(out_shape, tuple) else (out_shape,)
    moved = sum(a.size * a.dtype.itemsize for a in arrays) + sum(o.size * o.dtype.itemsize for o in outs)
    return pl.pallas_call(
        kernel,
        out_shape=out_shape,
        in_specs=[SMEM] * len(scalars) + [VMEM] * len(arrays),
        out_specs=tuple(VMEM for _ in outs) if isinstance(out_shape, tuple) else VMEM,
        scratch_shapes=scratch,
        compiler_params=pltpu.CompilerParams(vmem_limit_bytes=32 * 1024 * 1024),
        cost_estimate=pl.CostEstimate(flops=flops, bytes_accessed=moved, transcendentals=exps),
    )(*scalars, *arrays)


def on_device(queries, keys, values, out_grad, tile_counts, text_sample):
    text_rows, width = queries.shape
    rows = keys.shape[0]
    parts = lax.axis_size("tensor")
    devices = lax.axis_size("dp")
    groups = [[first + member for member in range(GROUP)] for first in range(0, devices, GROUP)]
    gather = functools.partial(lax.all_gather, axis_name="dp", axis_index_groups=groups)
    scalars = (lax.axis_index("dp").astype(jnp.int32).reshape(1), tile_counts, text_sample)
    heads = text_rows * width // HEAD_DIM
    matmul = 2 * heads * parts * rows * HEAD_DIM

    packed = jnp.stack([keys.reshape(rows, parts, HEAD_DIM), values.reshape(rows, parts, HEAD_DIM)])
    kv = lax.all_to_all(packed.transpose(2, 0, 1, 3), "tensor", 0, 0, tiled=True)
    q_all = gather(queries)
    g_all = gather(out_grad)
    stats = call(
        stats_kernel,
        jax.ShapeDtypeStruct((8, heads), jnp.float32),
        scalars,
        (q_all, g_all, kv),
        scratch=[pltpu.VMEM((parts * rows, heads), jnp.float32)],
        flops=2 * matmul,
        exps=heads * parts * rows,
    )
    stats_all = gather(stats)
    grads, dq = call(
        grads_kernel,
        (
            jax.ShapeDtypeStruct((parts, 2, rows, HEAD_DIM), jnp.bfloat16),
            jax.ShapeDtypeStruct((text_rows, width), jnp.bfloat16),
        ),
        scalars,
        (stats_all, q_all, g_all, kv),
        flops=5 * matmul,
        exps=heads * parts * rows,
    )
    back = lax.all_to_all(grads, "tensor", 0, 0, tiled=True)
    dq_all = gather(dq)
    query_grad = call(query_kernel, jax.ShapeDtypeStruct((text_rows, width), jnp.bfloat16), scalars, (dq_all,))
    back = back.transpose(1, 2, 0, 3).reshape(2, rows, parts * HEAD_DIM)
    return query_grad, back[0], back[1]


def solution(mesh):
    return jax.shard_map(
        on_device,
        mesh=mesh,
        in_specs=(
            P("dp", "tensor"),
            P(("dp", "tensor"), None),
            P(("dp", "tensor"), None),
            P("dp", "tensor"),
            P(),
            P(),
        ),
        out_specs=(P("dp", "tensor"), P(("dp", "tensor"), None), P(("dp", "tensor"), None)),
        check_vma=False,
    )
```

time: 154 us -> 82.3 us (0.53)
  starting transfers between devices: 85.9 us -> 13.7 us
  blocking collectives: 0 us -> 28.3 us
  other arithmetic: 13.6 us -> 1 us
  matrix products: 9.08 us -> 0 us
  Pallas kernels: 0 us -> 7.39 us
  waiting for transfers between devices: 32.4 us -> 25.8 us
  local copies, waits for them, and re-layouts: 9.24 us -> 4.19 us
  between operations: 3.11 us -> 0.72 us
    ppermute x18 -> x0, starting transfers between devices: 59.6 us -> none  [from_behind(): return lax.ppermute(block, axis, route)]
    all_gather x0 -> x4, blocking collectives: none -> 28.3 us  [the longest x1 8.18 us: on_device(): q_all = gather(queries)]
    all_to_all x4 -> x2, starting transfers between devices: 26.2 us -> 13.7 us  [the longest x1 10.2 us: on_device(): lax.all_to_all(packed.transpose(2, 0, 1, 3), 'tensor', 0, 0, tiled=True)]
    ppermute x18 -> x0, waiting for transfers between devices: 11.3 us -> none  [from_behind(): return lax.ppermute(block, axis, route)]
    dot_general x5 -> x0, matrix products: 9.08 us -> none  [the longest x1 4.69 us: slot_scores(): jnp.einsum('tkgd,rkd->kgtr', g_heads, v_heads, preferred_element_type=jnp...]
    pallas_call x0 -> x3, Pallas kernels: none -> 7.39 us  [call(): pl.pallas_call(kernel, out_shape=out_shape, in_specs=[SMEM] * len(scalars...]
    another operation x14 -> x0, other arithmetic: 7.05 us -> none
    all_to_all x4 -> x2, waiting for transfers between devices: 21.1 us -> 25.8 us  [the longest x1 16.3 us: on_device(): back = lax.all_to_all(grads, 'tensor', 0, 0, tiled=True)]
  transfers between devices with their start and end apart: 22 -> 2, of which waited for: 5 -> 2; matrix products, arithmetic and copies ran while one was open for 12% -> 0% of each run, Pallas kernels for 0% -> 2%
where the time goes in v1:
time: 82.3 us; the launch traced here: 81.1 us
  blocking collectives  28.3 us (34%)
  waiting for transfers between devices  25.8 us (31%)
  starting transfers between devices  13.7 us (17%)
  Pallas kernels  7.39 us (9%)
  local copies, waits for them, and re-layouts  4.19 us (5%)
  other arithmetic  1 us (1%)
    all_to_all x1, waiting for transfers between devices, on_device(): back = lax.all_to_all(grads, 'tensor', 0, 0, tiled=True)  16.3 us
    all_to_all x1, starting transfers between devices, on_device(): lax.all_to_all(packed.transpose(2, 0, 1, 3), 'tensor', 0, 0, tiled=True)  10.2 us
    all_to_all x1, waiting for transfers between devices, on_device(): lax.all_to_all(packed.transpose(2, 0, 1, 3), 'tensor', 0, 0, tiled=True)  9.5 us
    all_gather x1, blocking collectives, on_device(): q_all = gather(queries)  8.18 us
    pallas_call x3, Pallas kernels, call(): pl.pallas_call(kernel, out_shape=out_shape, in_specs=[SMEM] * len(scalars...  7.39 us
    all_gather x1, blocking collectives, on_device(): dq_all = gather(dq)  7.29 us
    all_gather x1, blocking collectives, on_device(): g_all = gather(out_grad)  7.28 us
    all_gather x1, blocking collectives, on_device(): stats_all = gather(stats)  5.57 us
  transfers between devices with their start and end apart: 2, of which 2 were waited for; matrix products, arithmetic and copies ran while one was open for 0% of the time, Pallas kernels for 2%

profile of v1, /device:TPU:7, one launch (start us, length us, event | category | flops | bytes accessed | tf_op | source)
XLA Modules:
  0.0 81.1 jit_solution(14041470417869136507)
XLA Ops:
  0.6 1.1 %copy.13 = bf16[26,8,8,128]{3,2,1,0:T(8,128)(2,1)S(1)} copy(bf16[26,8,8,128]{3,1,2,0:T(8,128)(2,1)} %bitcast.33) | data formatting | bytes 851968
  1.7 0.0 copy-start.2
  1.7 0.1 copy.9
  1.8 0.9 %copy-done.2 = bf16[208,1024]{1,0:T(8,128)(2,1)S(1)} copy-done((bf16[208,1024]{1,0:T(8,128)(2,1)S(1)}, bf16[208,1024]{1,0:T(8,128)(2,1)}, u32[]{:S(2)}) %copy-start.2) | copy-done | bytes 426008
  2.7 0.1 copy.14
  2.8 0.1 copy.10
  2.9 1.0 %maximum_bitcast_fusion = bf16[8,2,208,128]{3,2,1,0:T(8,128)(2,1)} fusion(bf16[1,208,8,128]{3,1,0,2:T(8,128)(2,1)S(1)} %copy.10, bf16[1,208,8,128]{3,1,0,2:T(8,128)(2,1)S(1)} %copy.9), kind=kLoop, calls=%fused_computation | loop fusion | flops 425984 | bytes 1703936 | tf_op jit(solution)/shard_map/transpose | solution.py:164
  3.9 0.0 copy-start.3
  3.9 10.2 %all-to-all-start = ((bf16[8,2,208,128]{3,2,1,0:T(8,128)(2,1)}), bf16[8,2,208,128]{3,2,1,0:T(8,128)(2,1)S(1)}, u32[]{:S(2)}, u32[]{:S(2)}) async-start(bf16[8,2,208,128]{3,2,1,0:T(8,128)(2,1)} %maximum_bitcast_fusion), calls=%async_computation | async-start | bytes 1703936 | tf_op jit(solution)/shard_map/all_to_all | solution.py:164
  14.0 0.0 copy-done.3
  14.0 0.0 copy-start.4
  14.1 8.2 %all-gather = bf16[512,512]{1,0:T(8,128)(2,1)S(1)} all-gather(bf16[128,512]{1,0:T(8,128)(2,1)S(1)} %copy-done.3), channel_id=2, replica_groups={{0,8,16,24},{32,40,48,56},{64,72,80,88},{96,104,112,120},{128,136,144,1..., dimensions={0}, use_global_device_ids=true | all-gather | bytes 655360 | tf_op jit(solution)/shard_map/all_gather | solution.py:165
  22.2 0.0 copy-done.4
  22.2 7.3 %all-gather.1 = bf16[512,512]{1,0:T(8,128)(2,1)S(1)} all-gather(bf16[128,512]{1,0:T(8,128)(2,1)S(1)} %copy-done.4), channel_id=3, replica_groups={{0,8,16,24},{32,40,48,56},{64,72,80,88},{96,104,112,120},{128,136,144,1..., dimensions={0}, use_global_device_ids=true | all-gather | bytes 655360 | tf_op jit(solution)/shard_map/all_gather | solution.py:166
  29.5 9.5 %all-to-all-done.kv_ref = bf16[8,2,208,128]{3,2,1,0:T(8,128)(2,1)S(1)} async-done(((bf16[8,2,208,128]{3,2,1,0:T(8,128)(2,1)}), bf16[8,2,208,128]{3,2,1,0:T(8,128)(2,1)S(1)}, u32[]{:S(2)}, u32[]{:S(2)}) %all-to-all-start) | async-done | bytes 852000 | tf_op jit(solution)/shard_map/all_to_all | solution.py:164
  39.0 0.0 copy-start
  39.0 0.0 copy-start.1
  39.0 0.7 copy-done
  39.7 0.0 copy-done.1
  39.7 2.0 %shard_map.85 = f32[8,512]{1,0:T(8,128)S(1)} custom-call(s32[1]{0:T(128)} %bitcast.dp_ref, s32[64]{0:T(128)S(1)} %copy-done, s32[64]{0:T(128)S(1)} %copy-done.1, bf16[4,128,512]{2,1,0:T(8,128)(2,1)S(1)} %bitcast.23, bf16[4,128,512]{2,1,0:T(8,128)(2,1)S(1)} %bitcast.25, bf16[8,2,208,128]{3,2,1,0:T(8,128)(2,1)S(1)} %all-to-all-done.kv_ref), custom_call_target="tpu_custom_call" | custom-call | flops 436207616 | bytes 1916928 | tf_op jit(solution)/shard_map/pallas_call | solution.py:141
  41.7 5.6 %all-gather.2 = f32[32,512]{1,0:T(8,128)S(1)} all-gather(f32[8,512]{1,0:T(8,128)S(1)} %shard_map.85), channel_id=4, replica_groups={{0,8,16,24},{32,40,48,56},{64,72,80,88},{96,104,112,120},{128,136,144,1..., dimensions={0}, use_global_device_ids=true | all-gather | bytes 81920 | tf_op jit(solution)/shard_map/all_gather | solution.py:176
  47.3 4.0 %shard_map.86 = (bf16[8,2,208,128]{3,2,1,0:T(8,128)(2,1)}, bf16[128,512]{1,0:T(8,128)(2,1)S(1)}) custom-call(s32[1]{0:T(128)} %bitcast.dp_ref, s32[64]{0:T(128)S(1)} %copy-done, s32[64]{0:T(128)S(1)} %copy-done.1, f32[4,8,512]{2,1,0:T(8,128)S(1)} %bitcast.27, bf16[4,128,512]{2,1,0:T(8,128)(2,1)S(1)} %bitcast.24, bf16[4,128,512]{2,1,0:T(8,128)(2,1)S(1)} %bitcast.26, ...), custom_call_target="tpu_custom_call" | custom-call | flops 1090519040 | bytes 2949120 | tf_op jit(solution)/shard_map/pallas_call | solution.py:141
  51.3 3.5 %all-to-all-start.1 = ((bf16[8,2,208,128]{3,2,1,0:T(8,128)(2,1)}), bf16[8,2,208,128]{3,2,1,0:T(8,128)(2,1)S(1)}, u32[]{:S(2)}, u32[]{:S(2)}) async-start(bf16[8,2,208,128]{3,2,1,0:T(8,128)(2,1)} %get-tuple-element.6), calls=%async_computation.1 | async-start | bytes 1703936 | tf_op jit(solution)/shard_map/all_to_all | solution.py:188
  54.9 7.3 %all-gather.3 = bf16[512,512]{1,0:T(8,128)(2,1)S(1)} all-gather(bf16[128,512]{1,0:T(8,128)(2,1)S(1)} %get-tuple-element.5), channel_id=5, replica_groups={{0,8,16,24},{32,40,48,56},{64,72,80,88},{96,104,112,120},{128,136,144,1..., dimensions={0}, use_global_device_ids=true | all-gather | bytes 655360 | tf_op jit(solution)/shard_map/all_gather | solution.py:189
  62.2 1.3 %shard_map.87 = bf16[128,512]{1,0:T(8,128)(2,1)} custom-call(s32[1]{0:T(128)} %bitcast.dp_ref, s32[64]{0:T(128)S(1)} %copy-done, s32[64]{0:T(128)S(1)} %copy-done.1, bf16[4,128,512]{2,1,0:T(8,128)(2,1)S(1)} %bitcast.22), custom_call_target="tpu_custom_call" | custom-call | bytes 655360 | tf_op jit(solution)/shard_map/pallas_call | solution.py:141
  63.5 16.3 %all-to-all-done.1 = bf16[8,2,208,128]{3,2,1,0:T(8,128)(2,1)S(1)} async-done(((bf16[8,2,208,128]{3,2,1,0:T(8,128)(2,1)}), bf16[8,2,208,128]{3,2,1,0:T(8,128)(2,1)S(1)}, u32[]{:S(2)}, u32[]{:S(2)}) %all-to-all-start.1) | async-done | bytes 852000 | tf_op jit(solution)/shard_map/all_to_all | solution.py:188
  79.8 0.1 fusion
  79.9 0.1 copy.12
  80.0 0.1 copy.11
  80.1 1.0 %copy_bitcast_fusion = (bf16[208,1024]{1,0:T(8,128)(2,1)}, bf16[208,1024]{1,0:T(8,128)(2,1)}) fusion(bf16[26,8,8,128]{3,2,1,0:T(8,128)(2,1)S(1)} %bitcast.31, bf16[26,8,8,128]{3,2,1,0:T(8,128)(2,1)S(1)} %bitcast.32), kind=kLoop, calls=%fused_computation.1 | loop fusion | bytes 1703936 | tf_op jit(solution)/shard_map/squeeze | solution.py:192
Async XLA Ops:
  1.7 1.0 %copy-start.2 = (bf16[208,1024]{1,0:T(8,128)(2,1)S(1)}, bf16[208,1024]{1,0:T(8,128)(2,1)}, u32[]{:S(2)}) copy-start(bf16[208,1024]{1,0:T(8,128)(2,1)} %param.8) | copy-start | bytes 1277956
  3.9 10.2 %copy-start.3 = (bf16[128,512]{1,0:T(8,128)(2,1)S(1)}, bf16[128,512]{1,0:T(8,128)(2,1)}, u32[]{:S(2)}) copy-start(bf16[128,512]{1,0:T(8,128)(2,1)} %param.6) | copy-start | bytes 393220
  3.9 35.1 %all-to-all-start = ((bf16[8,2,208,128]{3,2,1,0:T(8,128)(2,1)}), bf16[8,2,208,128]{3,2,1,0:T(8,128)(2,1)S(1)}, u32[]{:S(2)}, u32[]{:S(2)}) async-start(bf16[8,2,208,128]{3,2,1,0:T(8,128)(2,1)} %maximum_bitcast_fusion), calls=%async_computation | async-start | bytes 1703936 | tf_op jit(solution)/shard_map/all_to_all | solution.py:164
  14.0 8.2 %copy-start.4 = (bf16[128,512]{1,0:T(8,128)(2,1)S(1)}, bf16[128,512]{1,0:T(8,128)(2,1)}, u32[]{:S(2)}) copy-start(bf16[128,512]{1,0:T(8,128)(2,1)} %param.9) | copy-start | bytes 393220
  39.0 0.7 copy-start
  39.0 0.7 copy-start.1
  51.3 28.5 %all-to-all-start.1 = ((bf16[8,2,208,128]{3,2,1,0:T(8,128)(2,1)}), bf16[8,2,208,128]{3,2,1,0:T(8,128)(2,1)S(1)}, u32[]{:S(2)}, u32[]{:S(2)}) async-start(bf16[8,2,208,128]{3,2,1,0:T(8,128)(2,1)} %get-tuple-element.6), calls=%async_computation.1 | async-start | bytes 1703936 | tf_op jit(solution)/shard_map/all_to_all | solution.py:188

commit v2 on v1

v2 whole, which is shorter than its diff:
```python
import functools
import math

import jax
import jax.numpy as jnp
from jax import lax
from jax.experimental import pallas as pl
from jax.experimental.pallas import tpu as pltpu
from jax.sharding import PartitionSpec as P

HEAD_DIM = 128
TILE_ROWS = 1601
GROUP = 4
SCALE = HEAD_DIM ** -0.5
LOG2E = 1.4426950408889634
SCALE2 = SCALE * LOG2E


def owners(dp, counts, text):
    first = (dp // GROUP) * GROUP
    end0 = counts[first]
    end1 = end0 + counts[first + 1]
    end2 = end1 + counts[first + 2]
    found = []
    for slot in range(GROUP):
        sample = first
        for end in (end0, end1, end2):
            sample = sample + jnp.where(end <= slot, 1, 0)
        owner = jnp.int32(0)
        for member in range(1, GROUP):
            owner = owner + jnp.where(text[first + member] == sample, member, 0)
        found.append(owner)
    return found, dp - first


def pick(options, position):
    chosen = options[0]
    for index in range(1, GROUP):
        chosen = jnp.where(position == index, options[index], chosen)
    return chosen


def head_rows(block):
    heads = block.shape[1] // HEAD_DIM
    return jnp.concatenate([block[:, h * HEAD_DIM:(h + 1) * HEAD_DIM] for h in range(heads)], axis=0)


def member_order(size):
    return [(size - 1 + index) % size for index in range(size)]


def pack_kernel(order, keys_ref, values_ref, out_ref, held, in_sems, out_sems):
    parts = out_ref.shape[0]
    loads = []
    for part in range(parts):
        for side, ref in enumerate((keys_ref, values_ref)):
            columns = ref.at[:, pl.ds(order[part] * HEAD_DIM, HEAD_DIM)]
            loads.append(pltpu.make_async_copy(columns, held.at[part, side], in_sems.at[part, side]))
            loads[-1].start()
    stores = []
    for part in range(parts):
        loads[2 * part].wait()
        loads[2 * part + 1].wait()
        stores.append(pltpu.make_async_copy(held.at[part], out_ref.at[part], out_sems.at[part]))
        stores[-1].start()
    for store in stores:
        store.wait()


def unpack_kernel(order, in_ref, keys_ref, values_ref, sems):
    copies = []
    for side, ref in enumerate((keys_ref, values_ref)):
        for part in range(in_ref.shape[0]):
            columns = ref.at[:, pl.ds(order[part] * HEAD_DIM, HEAD_DIM)]
            copies.append(pltpu.make_async_copy(in_ref.at[part, side], columns, sems.at[part, side]))
    for copy in copies:
        copy.start()
    for copy in copies:
        copy.wait()


def text_kernel(dp_ref, counts_ref, text_ref, q_ref, g_ref, flag_ref, qt_ref, gt_ref, q_out_ref, g_out_ref):
    found, position = owners(dp_ref[0], counts_ref, text_ref)
    mine = pick(found, position)
    for ref, out_ref, turned_ref in ((q_ref, q_out_ref, qt_ref), (g_ref, g_out_ref, gt_ref)):
        rows = head_rows(ref[mine])
        out_ref[...] = rows
        turned_ref[...] = rows.T
    for slot in range(GROUP):
        line = jnp.zeros((1, flag_ref.shape[1]), jnp.float32)
        flag_ref[slot:slot + 1] = line + jnp.where(found[slot] == mine, 1.0, 0.0)
        flag_ref[GROUP + slot:GROUP + slot + 1] = line + jnp.where(found[slot] == position, 1.0, 0.0)


def stats_kernel(order, qt_ref, gt_ref, kv_ref, stat_ref, weight_ref, grad_ref):
    parts, rows = kv_ref.shape[0], kv_ref.shape[2]
    q_turned, g_turned = qt_ref[...], gt_ref[...]
    top = None
    for part in range(parts):
        scores = jnp.dot(kv_ref[part, 0], q_turned, preferred_element_type=jnp.float32) * SCALE2
        if (order[part] + 1) * rows > TILE_ROWS:
            row = lax.broadcasted_iota(jnp.int32, scores.shape, 0) + order[part] * rows
            scores = jnp.where(row < TILE_ROWS, scores, -1e30)
        weight_ref[pl.ds(part * rows, rows), :] = scores
        part_top = jnp.max(scores, axis=0, keepdims=True)
        top = part_top if top is None else jnp.maximum(top, part_top)
    total = jnp.zeros_like(top)
    product = jnp.zeros_like(top)
    for part in range(parts):
        span = pl.ds(part * rows, rows)
        weights = jnp.exp2(weight_ref[span, :] - top)
        weight_ref[span, :] = weights
        grads = jnp.dot(kv_ref[part, 1], g_turned, preferred_element_type=jnp.float32)
        grad_ref[span, :] = grads
        total = total + jnp.sum(weights, axis=0, keepdims=True)
        product = product + jnp.sum(weights * grads, axis=0, keepdims=True)
    stat_ref[...] = jnp.concatenate([top, total, product, jnp.zeros((5, top.shape[1]), jnp.float32)], axis=0)


def grads_kernel(
    flag_ref, all_ref, own_ref, q_ref, g_ref, kv_ref, weight_ref, grad_ref, out_ref, dq_ref, held, sems
):
    tops = [jnp.where(flag_ref[slot:slot + 1] > 0, all_ref[slot][0:1], -1e30) for slot in range(GROUP)]
    top = functools.reduce(jnp.maximum, tops)
    total = jnp.zeros_like(top)
    product = jnp.zeros_like(top)
    for slot in range(GROUP):
        share = jnp.where(flag_ref[slot:slot + 1] > 0, jnp.exp2(tops[slot] - top), 0.0)
        total = total + share * all_ref[slot][1:2]
        product = product + share * all_ref[slot][2:3]
    delta = product / total
    rescale = jnp.exp2(own_ref[0:1] - top) / total
    parts, rows = kv_ref.shape[0], kv_ref.shape[2]
    q_rows, g_rows = q_ref[...], g_ref[...]
    dq = None
    copies = []
    for part in range(parts):
        span = pl.ds(part * rows, rows)
        probs = weight_ref[span, :] * rescale
        dscore = (probs * (grad_ref[span, :] - delta)).astype(jnp.bfloat16)
        probs = probs.astype(jnp.bfloat16)
        held[part, 0] = (jnp.dot(dscore, q_rows, preferred_element_type=jnp.float32) * SCALE).astype(jnp.bfloat16)
        held[part, 1] = jnp.dot(probs, g_rows, preferred_element_type=jnp.float32).astype(jnp.bfloat16)
        copies.append(pltpu.make_async_copy(held.at[part], out_ref.at[part], sems.at[part]))
        copies[-1].start()
        query_part = lax.dot_general(
            kv_ref[part, 0], dscore, (((0,), (0,)), ((), ())), preferred_element_type=jnp.float32
        )
        dq = query_part if dq is None else dq + query_part
    for head in range(dq.shape[1] // HEAD_DIM):
        cols = slice(head * HEAD_DIM, (head + 1) * HEAD_DIM)
        dq_ref[:, cols] = (dq[:, cols].T * SCALE).astype(jnp.bfloat16)
    for copy in copies:
        copy.wait()


def query_kernel(flag_ref, parts_ref, out_ref):
    total = jnp.zeros(out_ref.shape, jnp.float32)
    for slot in range(GROUP):
        flag = flag_ref[GROUP + slot:GROUP + slot + 1]
        total = total + jnp.where(flag > 0, parts_ref[slot].astype(jnp.float32), 0.0)
    out_ref[...] = total.astype(jnp.bfloat16)


SMEM = pl.BlockSpec(memory_space=pltpu.SMEM)
VMEM = pl.BlockSpec(memory_space=pltpu.VMEM)
ANY = pl.BlockSpec(memory_space=pl.ANY)
MIB = 1024 * 1024


def call(kernel, out_shape, out_specs, in_specs, args, scratch=(), limit=32, flops=0, exps=0):
    outs = out_shape if isinstance(out_shape, tuple) else (out_shape,)
    moved = sum(a.size * a.dtype.itemsize for a in args) + sum(math.prod(o.shape) * 2 for o in outs)
    return pl.pallas_call(
        kernel,
        out_shape=out_shape,
        in_specs=in_specs,
        out_specs=out_specs,
        scratch_shapes=scratch,
        compiler_params=pltpu.CompilerParams(vmem_limit_bytes=limit * MIB),
        cost_estimate=pl.CostEstimate(flops=flops, bytes_accessed=moved, transcendentals=exps),
    )(*args)


def on_device(queries, keys, values, out_grad, tile_counts, text_sample):
    text_rows, width = queries.shape
    rows = keys.shape[0]
    parts = lax.axis_size("tensor")
    order = member_order(parts)
    exchange = functools.partial(
        lax.all_to_all, axis_name="tensor", split_axis=0, concat_axis=0, axis_index_groups=[order], tiled=True
    )
    devices = lax.axis_size("dp")
    groups = [[first + member for member in range(GROUP)] for first in range(0, devices, GROUP)]
    gather = functools.partial(lax.all_gather, axis_name="dp", axis_index_groups=groups)
    position = lax.axis_index("dp").astype(jnp.int32).reshape(1)
    heads = text_rows * width // HEAD_DIM
    matmul = 2 * heads * parts * rows * HEAD_DIM
    half = jnp.bfloat16
    full = jnp.float32
    blocks = (parts, 2, rows, HEAD_DIM)

    packed = call(
        functools.partial(pack_kernel, order),
        jax.ShapeDtypeStruct(blocks, half),
        ANY,
        [ANY, ANY],
        (keys, values),
        scratch=[
            pltpu.VMEM(blocks, half),
            pltpu.SemaphoreType.DMA((parts, 2)),
            pltpu.SemaphoreType.DMA((parts,)),
        ],
        limit=60,
    )
    kv = exchange(packed)
    q_all = gather(queries)
    g_all = gather(out_grad)
    flags, q_turned, g_turned, q_rows, g_rows = call(
        text_kernel,
        (
            pltpu.VMEM((2 * GROUP, heads), full),
            pltpu.VMEM((HEAD_DIM, heads), half),
            pltpu.VMEM((HEAD_DIM, heads), half),
            pltpu.VMEM((heads, HEAD_DIM), half),
            pltpu.VMEM((heads, HEAD_DIM), half),
        ),
        (VMEM,) * 5,
        [SMEM] * 3 + [VMEM] * 2,
        (position, tile_counts, text_sample, q_all, g_all),
    )
    stats, weights, grad_prod = call(
        functools.partial(stats_kernel, order),
        (
            pltpu.VMEM((8, heads), full),
            pltpu.VMEM((parts * rows, heads), full),
            pltpu.VMEM((parts * rows, heads), full),
        ),
        (VMEM,) * 3,
        [VMEM] * 3,
        (q_turned, g_turned, kv),
        flops=2 * matmul,
        exps=heads * parts * rows,
    )
    stats_all = gather(stats)
    grads, dq = call(
        grads_kernel,
        (jax.ShapeDtypeStruct(blocks, half), pltpu.VMEM((text_rows, width), half)),
        (ANY, VMEM),
        [VMEM] * 8,
        (flags, stats_all, stats, q_rows, g_rows, kv, weights, grad_prod),
        scratch=[pltpu.VMEM(blocks, half), pltpu.SemaphoreType.DMA((parts,))],
        flops=3 * matmul,
    )
    back = exchange(grads)
    dq_all = gather(dq)
    query_grad = call(
        query_kernel, jax.ShapeDtypeStruct((text_rows, width), half), VMEM, [VMEM] * 2, (flags, dq_all)
    )
    tile = jax.ShapeDtypeStruct((rows, parts * HEAD_DIM), half)
    key_grad, value_grad = call(
        functools.partial(unpack_kernel, order),
        (tile, tile),
        (ANY, ANY),
        [ANY],
        (back,),
        scratch=[pltpu.SemaphoreType.DMA((parts, 2))],
        limit=8,
    )
    return query_grad, key_grad, value_grad


def solution(mesh):
    return jax.shard_map(
        on_device,
        mesh=mesh,
        in_specs=(
            P("dp", "tensor"),
            P(("dp", "tensor"), None),
            P(("dp", "tensor"), None),
            P("dp", "tensor"),
            P(),
            P(),
        ),
        out_specs=(P("dp", "tensor"), P(("dp", "tensor"), None), P(("dp", "tensor"), None)),
        check_vma=False,
    )
```

time: 82.3 us -> 73.3 us (0.89)
  waiting for transfers between devices: 25.8 us -> 15.6 us
  starting transfers between devices: 13.7 us -> 18.3 us
  local copies, waits for them, and re-layouts: 4.19 us -> 0.02 us
  blocking collectives: 28.3 us -> 29.7 us
  other arithmetic: 1 us -> 0 us
    all_to_all x2, waiting for transfers between devices: 25.8 us -> 15.6 us  [the longest x1 11.8 us: on_device(): back = exchange(grads)]
    all_to_all x2, starting transfers between devices: 13.7 us -> 18.3 us  [the longest x1 12.2 us: on_device(): kv = exchange(packed)]
    unnamed x12 -> x8, local copies, waits for them, and re-layouts: 2.75 us -> 0.02 us
    all_gather x1, blocking collectives: 5.57 us -> 6.87 us  [on_device(): stats_all = gather(stats)]
    squeeze x1 -> x0, local copies, waits for them, and re-layouts: 1.04 us -> none  [on_device(): return (query_grad, back[0], back[1])]
    transpose x1 -> x0, other arithmetic: 1 us -> none  [on_device(): packed.transpose(2, 0, 1, 3)]
    pallas_call x3 -> x6, Pallas kernels: 7.39 us -> 7.95 us  [call(): pl.pallas_call(kernel, out_shape=out_shape, in_specs=in_specs, out_specs=...]
where the time goes in v2:
time: 73.3 us; the launch traced here: 72.2 us
  blocking collectives  29.7 us (41%)
  starting transfers between devices  18.3 us (25%)
  waiting for transfers between devices  15.6 us (21%)
  Pallas kernels  7.95 us (11%)
    all_to_all x1, starting transfers between devices, on_device(): kv = exchange(packed)  12.2 us
    all_to_all x1, waiting for transfers between devices, on_device(): back = exchange(grads)  11.8 us
    all_gather x1, blocking collectives, on_device(): q_all = gather(queries)  8.03 us
    pallas_call x6, Pallas kernels, call(): pl.pallas_call(kernel, out_shape=out_shape, in_specs=in_specs, out_specs=...  7.95 us
    all_gather x1, blocking collectives, on_device(): dq_all = gather(dq)  7.54 us
    all_gather x1, blocking collectives, on_device(): g_all = gather(out_grad)  7.28 us
    all_gather x1, blocking collectives, on_device(): stats_all = gather(stats)  6.87 us
    all_to_all x1, starting transfers between devices, on_device(): back = exchange(grads)  6.05 us
  transfers between devices with their start and end apart: 2, of which 2 were waited for; matrix products, arithmetic and copies ran while one was open for 0% of the time, Pallas kernels for 2%

profile of v2, /device:TPU:7, one launch (start us, length us, event | category | flops | bytes accessed | tf_op | source)
XLA Modules:
  0.0 72.2 jit_solution(3548566235827412210)
XLA Ops:
  0.6 0.0 copy-start.2
  0.6 0.0 copy-start.3
  0.7 0.0 copy-start.1
  0.7 0.0 copy-start
  0.7 2.1 %shard_map.86 = bf16[8,2,208,128]{3,2,1,0:T(8,128)(2,1)} custom-call(bf16[208,1024]{1,0:T(8,128)(2,1)} %keys_ref.1, bf16[208,1024]{1,0:T(8,128)(2,1)} %values_ref.1), custom_call_target="tpu_custom_call" | custom-call | bytes 1703936 | tf_op jit(solution)/shard_map/pallas_call | solution.py:174
  2.8 12.2 %all-to-all-start = ((bf16[8,2,208,128]{3,2,1,0:T(8,128)(2,1)}), bf16[8,2,208,128]{3,2,1,0:T(8,128)(2,1)S(1)}, u32[]{:S(2)}, u32[]{:S(2)}) async-start(bf16[8,2,208,128]{3,2,1,0:T(8,128)(2,1)} %shard_map.86), calls=%async_computation | async-start | bytes 1703936 | tf_op jit(solution)/shard_map/all_to_all | solution.py:216
  15.0 0.0 copy-done.2
  15.0 8.0 %all-gather = bf16[512,512]{1,0:T(8,128)(2,1)S(1)} all-gather(bf16[128,512]{1,0:T(8,128)(2,1)S(1)} %copy-done.2), channel_id=2, replica_groups={{0,8,16,24},{32,40,48,56},{64,72,80,88},{96,104,112,120},{128,136,144,1..., dimensions={0}, use_global_device_ids=true | all-gather | bytes 655360 | tf_op jit(solution)/shard_map/all_gather | solution.py:217
  23.0 0.0 copy-done.3
  23.1 7.3 %all-gather.1 = bf16[512,512]{1,0:T(8,128)(2,1)S(1)} all-gather(bf16[128,512]{1,0:T(8,128)(2,1)S(1)} %copy-done.3), channel_id=3, replica_groups={{0,8,16,24},{32,40,48,56},{64,72,80,88},{96,104,112,120},{128,136,144,1..., dimensions={0}, use_global_device_ids=true | all-gather | bytes 655360 | tf_op jit(solution)/shard_map/all_gather | solution.py:218
  30.3 0.0 copy-done.1
  30.3 0.0 copy-done
  30.3 0.7 shard_map.85
  31.0 3.8 %all-to-all-done.kv_ref = bf16[8,2,208,128]{3,2,1,0:T(8,128)(2,1)S(1)} async-done(((bf16[8,2,208,128]{3,2,1,0:T(8,128)(2,1)}), bf16[8,2,208,128]{3,2,1,0:T(8,128)(2,1)S(1)}, u32[]{:S(2)}, u32[]{:S(2)}) %all-to-all-start) | async-done | bytes 852000 | tf_op jit(solution)/shard_map/all_to_all | solution.py:216
  34.8 1.3 %shard_map.87 = (f32[8,512]{1,0:T(8,128)S(1)}, f32[1664,512]{1,0:T(8,128)S(1)}, f32[1664,512]{1,0:T(8,128)S(1)}) custom-call(bf16[128,512]{1,0:T(8,128)(2,1)S(1)} %get-tuple-element.16.qt_ref, bf16[128,512]{1,0:T(8,128)(2,1)S(1)} %get-tuple-element.17.gt_ref, bf16[8,2,208,128]{3,2,1,0:T(8,128)(2,1)S(1)} %all-to-all-done.kv_ref), custom_call_target="tpu_custom_call" | custom-call | flops 436207616 | bytes 4530176 | tf_op jit(solution)/shard_map/pallas_call | solution.py:174
  36.1 6.9 %all-gather.2 = f32[32,512]{1,0:T(8,128)S(1)} all-gather(f32[8,512]{1,0:T(8,128)S(1)} %get-tuple-element.18.own_ref), channel_id=4, replica_groups={{0,8,16,24},{32,40,48,56},{64,72,80,88},{96,104,112,120},{128,136,144,1..., dimensions={0}, use_global_device_ids=true | all-gather | bytes 81920 | tf_op jit(solution)/shard_map/all_gather | solution.py:245
  43.0 2.1 %shard_map.88 = (bf16[8,2,208,128]{3,2,1,0:T(8,128)(2,1)}, bf16[128,512]{1,0:T(8,128)(2,1)S(1)}) custom-call(f32[8,512]{1,0:T(8,128)S(1)} %get-tuple-element.15.flag_ref, f32[4,8,512]{2,1,0:T(8,128)S(1)} %bitcast.8, f32[8,512]{1,0:T(8,128)S(1)} %get-tuple-element.18.own_ref, bf16[512,128]{1,0:T(8,128)(2,1)S(1)} %get-tuple-element.19.q_ref, ...), custom_call_target="tpu_custom_call" | custom-call | flops 654311424 | bytes 9011200 | tf_op jit(solution)/shard_map/pallas_call | solution.py:174
  45.0 6.1 %all-to-all-start.1 = ((bf16[8,2,208,128]{3,2,1,0:T(8,128)(2,1)}), bf16[8,2,208,128]{3,2,1,0:T(8,128)(2,1)S(1)}, u32[]{:S(2)}, u32[]{:S(2)}) async-start(bf16[8,2,208,128]{3,2,1,0:T(8,128)(2,1)} %get-tuple-element.24), calls=%async_computation.1 | async-start | bytes 1703936 | tf_op jit(solution)/shard_map/all_to_all | solution.py:255
  51.1 7.5 %all-gather.3 = bf16[512,512]{1,0:T(8,128)(2,1)S(1)} all-gather(bf16[128,512]{1,0:T(8,128)(2,1)S(1)} %get-tuple-element.23), channel_id=5, replica_groups={{0,8,16,24},{32,40,48,56},{64,72,80,88},{96,104,112,120},{128,136,144,1..., dimensions={0}, use_global_device_ids=true | all-gather | bytes 655360 | tf_op jit(solution)/shard_map/all_gather | solution.py:256
  58.6 0.8 %shard_map.89 = bf16[128,512]{1,0:T(8,128)(2,1)} custom-call(f32[8,512]{1,0:T(8,128)S(1)} %get-tuple-element.15.flag_ref, bf16[4,128,512]{2,1,0:T(8,128)(2,1)S(1)} %bitcast.7), custom_call_target="tpu_custom_call" | custom-call | bytes 671744 | tf_op jit(solution)/shard_map/pallas_call | solution.py:174
  59.4 11.8 %all-to-all-done.1.in_ref = bf16[8,2,208,128]{3,2,1,0:T(8,128)(2,1)S(1)} async-done(((bf16[8,2,208,128]{3,2,1,0:T(8,128)(2,1)}), bf16[8,2,208,128]{3,2,1,0:T(8,128)(2,1)S(1)}, u32[]{:S(2)}, u32[]{:S(2)}) %all-to-all-start.1) | async-done | bytes 852000 | tf_op jit(solution)/shard_map/all_to_all | solution.py:255
  71.2 1.0 %shard_map.90 = (bf16[208,1024]{1,0:T(8,128)(2,1)}, bf16[208,1024]{1,0:T(8,128)(2,1)}) custom-call(bf16[8,2,208,128]{3,2,1,0:T(8,128)(2,1)S(1)} %all-to-all-done.1.in_ref), custom_call_target="tpu_custom_call" | custom-call | bytes 1703936 | tf_op jit(solution)/shard_map/pallas_call | solution.py:174
Async XLA Ops:
  0.6 14.4 %copy-start.2 = (bf16[128,512]{1,0:T(8,128)(2,1)S(1)}, bf16[128,512]{1,0:T(8,128)(2,1)}, u32[]{:S(2)}) copy-start(bf16[128,512]{1,0:T(8,128)(2,1)} %param.6) | copy-start | bytes 393220
  0.6 22.4 %copy-start.3 = (bf16[128,512]{1,0:T(8,128)(2,1)S(1)}, bf16[128,512]{1,0:T(8,128)(2,1)}, u32[]{:S(2)}) copy-start(bf16[128,512]{1,0:T(8,128)(2,1)} %param.9) | copy-start | bytes 393220
  0.7 29.7 %copy-start.1 = (s32[64]{0:T(128)S(1)}, s32[64]{0:T(128)}, u32[]{:S(2)}) copy-start(s32[64]{0:T(128)} %text_ref.1) | copy-start | bytes 772
  0.7 29.7 %copy-start = (s32[64]{0:T(128)S(1)}, s32[64]{0:T(128)}, u32[]{:S(2)}) copy-start(s32[64]{0:T(128)} %counts_ref.1) | copy-start | bytes 772
  2.8 32.0 %all-to-all-start = ((bf16[8,2,208,128]{3,2,1,0:T(8,128)(2,1)}), bf16[8,2,208,128]{3,2,1,0:T(8,128)(2,1)S(1)}, u32[]{:S(2)}, u32[]{:S(2)}) async-start(bf16[8,2,208,128]{3,2,1,0:T(8,128)(2,1)} %shard_map.86), calls=%async_computation | async-start | bytes 1703936 | tf_op jit(solution)/shard_map/all_to_all | solution.py:216
  45.0 26.2 %all-to-all-start.1 = ((bf16[8,2,208,128]{3,2,1,0:T(8,128)(2,1)}), bf16[8,2,208,128]{3,2,1,0:T(8,128)(2,1)S(1)}, u32[]{:S(2)}, u32[]{:S(2)}) async-start(bf16[8,2,208,128]{3,2,1,0:T(8,128)(2,1)} %get-tuple-element.24), calls=%async_computation.1 | async-start | bytes 1703936 | tf_op jit(solution)/shard_map/all_to_all | solution.py:255

commit v3 on v2

--- a/solution.py
+++ b/solution.py
@@ -45,8 +45,8 @@
     return jnp.concatenate([block[:, h * HEAD_DIM:(h + 1) * HEAD_DIM] for h in range(heads)], axis=0)
 
 
-def member_order(size):
-    return [(size - 1 + index) % size for index in range(size)]
+def member_order(first, size):
+    return [(first + index) % size for index in range(size)]
 
 
 def pack_kernel(order, keys_ref, values_ref, out_ref, held, in_sems, out_sems):
@@ -117,9 +117,7 @@
     stat_ref[...] = jnp.concatenate([top, total, product, jnp.zeros((5, top.shape[1]), jnp.float32)], axis=0)
 
 
-def grads_kernel(
-    flag_ref, all_ref, own_ref, q_ref, g_ref, kv_ref, weight_ref, grad_ref, out_ref, dq_ref, held, sems
-):
+def merged(flag_ref, all_ref):
     tops = [jnp.where(flag_ref[slot:slot + 1] > 0, all_ref[slot][0:1], -1e30) for slot in range(GROUP)]
     top = functools.reduce(jnp.maximum, tops)
     total = jnp.zeros_like(top)
@@ -128,30 +126,46 @@
         share = jnp.where(flag_ref[slot:slot + 1] > 0, jnp.exp2(tops[slot] - top), 0.0)
         total = total + share * all_ref[slot][1:2]
         product = product + share * all_ref[slot][2:3]
-    delta = product / total
-    rescale = jnp.exp2(own_ref[0:1] - top) / total
-    parts, rows = kv_ref.shape[0], kv_ref.shape[2]
+    return top, 1.0 / total, product / total
+
+
+def grads_kernel(
+    places, flag_ref, all_ref, own_ref, q_ref, g_ref, weight_ref, grad_ref, out_ref, dscore_ref, held, sems
+):
+    top, inverse, delta = merged(flag_ref, all_ref)
+    rescale = jnp.exp2(own_ref[0:1] - top) * inverse
+    parts, rows = out_ref.shape[0], out_ref.shape[2]
     q_rows, g_rows = q_ref[...], g_ref[...]
-    dq = None
     copies = []
     for part in range(parts):
         span = pl.ds(part * rows, rows)
         probs = weight_ref[span, :] * rescale
         dscore = (probs * (grad_ref[span, :] - delta)).astype(jnp.bfloat16)
+        dscore_ref[span, :] = dscore
         probs = probs.astype(jnp.bfloat16)
-        held[part, 0] = (jnp.dot(dscore, q_rows, preferred_element_type=jnp.float32) * SCALE).astype(jnp.bfloat16)
-        held[part, 1] = jnp.dot(probs, g_rows, preferred_element_type=jnp.float32).astype(jnp.bfloat16)
-        copies.append(pltpu.make_async_copy(held.at[part], out_ref.at[part], sems.at[part]))
+        place = places[part]
+        held[place, 0] = (jnp.dot(dscore, q_rows, preferred_element_type=jnp.float32) * SCALE).astype(jnp.bfloat16)
+        held[place, 1] = jnp.dot(probs, g_rows, preferred_element_type=jnp.float32).astype(jnp.bfloat16)
+        copies.append(pltpu.make_async_copy(held.at[place], out_ref.at[place], sems.at[part]))
         copies[-1].start()
+    for copy in copies:
+        copy.wait()
+
+
+def text_grad_kernel(kv_ref, dscore_ref, dq_ref):
+    parts, rows = kv_ref.shape[0], kv_ref.shape[2]
+    dq = None
+    for part in range(parts):
         query_part = lax.dot_general(
-            kv_ref[part, 0], dscore, (((0,), (0,)), ((), ())), preferred_element_type=jnp.float32
+            kv_ref[part, 0],
+            dscore_ref[pl.ds(part * rows, rows), :],
+            (((0,), (0,)), ((), ())),
+            preferred_element_type=jnp.float32,
         )
         dq = query_part if dq is None else dq + query_part
     for head in range(dq.shape[1] // HEAD_DIM):
         cols = slice(head * HEAD_DIM, (head + 1) * HEAD_DIM)
         dq_ref[:, cols] = (dq[:, cols].T * SCALE).astype(jnp.bfloat16)
-    for copy in copies:
-        copy.wait()
 
 
 def query_kernel(flag_ref, parts_ref, out_ref):
@@ -164,6 +178,7 @@
 
 SMEM = pl.BlockSpec(memory_space=pltpu.SMEM)
 VMEM = pl.BlockSpec(memory_space=pltpu.VMEM)
+HBM = pl.BlockSpec(memory_space=pltpu.HBM)
 ANY = pl.BlockSpec(memory_space=pl.ANY)
 MIB = 1024 * 1024
 
@@ -186,10 +201,9 @@
     text_rows, width = queries.shape
     rows = keys.shape[0]
     parts = lax.axis_size("tensor")
-    order = member_order(parts)
-    exchange = functools.partial(
-        lax.all_to_all, axis_name="tensor", split_axis=0, concat_axis=0, axis_index_groups=[order], tiled=True
-    )
+    order = member_order(parts - 2, parts)
+    back_order = member_order(parts - 3, parts)
+    exchange = functools.partial(lax.all_to_all, axis_name="tensor", split_axis=0, concat_axis=0, tiled=True)
     devices = lax.axis_size("dp")
     groups = [[first + member for member in range(GROUP)] for first in range(0, devices, GROUP)]
     gather = functools.partial(lax.all_gather, axis_name="dp", axis_index_groups=groups)
@@ -202,8 +216,8 @@
 
     packed = call(
         functools.partial(pack_kernel, order),
-        jax.ShapeDtypeStruct(blocks, half),
-        ANY,
+        pltpu.HBM(blocks, half),
+        HBM,
         [ANY, ANY],
         (keys, values),
         scratch=[
@@ -213,7 +227,7 @@
         ],
         limit=60,
     )
-    kv = exchange(packed)
+    kv = exchange(packed, axis_index_groups=[order])
     q_all = gather(queries)
     g_all = gather(out_grad)
     flags, q_turned, g_turned, q_rows, g_rows = call(
@@ -243,23 +257,31 @@
         exps=heads * parts * rows,
     )
     stats_all = gather(stats)
-    grads, dq = call(
-        grads_kernel,
-        (jax.ShapeDtypeStruct(blocks, half), pltpu.VMEM((text_rows, width), half)),
-        (ANY, VMEM),
-        [VMEM] * 8,
-        (flags, stats_all, stats, q_rows, g_rows, kv, weights, grad_prod),
+    grads, dscore = call(
+        functools.partial(grads_kernel, [back_order.index(member) for member in order]),
+        (pltpu.HBM(blocks, half), pltpu.VMEM((parts * rows, heads), half)),
+        (HBM, VMEM),
+        [VMEM] * 7,
+        (flags, stats_all, stats, q_rows, g_rows, weights, grad_prod),
         scratch=[pltpu.VMEM(blocks, half), pltpu.SemaphoreType.DMA((parts,))],
-        flops=3 * matmul,
-    )
-    back = exchange(grads)
+        flops=2 * matmul,
+    )
+    back = exchange(grads, axis_index_groups=[back_order])
+    dq = call(
+        text_grad_kernel,
+        pltpu.VMEM((text_rows, width), half),
+        VMEM,
+        [VMEM] * 2,
+        (kv, dscore),
+        flops=matmul,
+    )
     dq_all = gather(dq)
     query_grad = call(
         query_kernel, jax.ShapeDtypeStruct((text_rows, width), half), VMEM, [VMEM] * 2, (flags, dq_all)
     )
     tile = jax.ShapeDtypeStruct((rows, parts * HEAD_DIM), half)
     key_grad, value_grad = call(
-        functools.partial(unpack_kernel, order),
+        functools.partial(unpack_kernel, back_order),
         (tile, tile),
         (ANY, ANY),
         [ANY],

time: 73.3 us -> 72.1 us (0.984)
  waiting for transfers between devices: 15.6 us -> 11.9 us
  starting transfers between devices: 18.3 us -> 20.6 us
    all_to_all x2, waiting for transfers between devices: 15.6 us -> 11.9 us  [the longest x1 9.26 us: on_device(): back = exchange(grads, axis_index_groups=[back_order])]
    all_to_all x2, starting transfers between devices: 18.3 us -> 20.6 us  [the longest x1 12.2 us: on_device(): kv = exchange(packed, axis_index_groups=[order])]
    pallas_call x6 -> x7, Pallas kernels: 7.95 us -> 8.35 us  [call(): pl.pallas_call(kernel, out_shape=out_shape, in_specs=in_specs, out_specs=...]
  transfers between devices with their start and end apart: 2 -> 2, of which waited for: 2 -> 2; matrix products, arithmetic and copies ran while one was open for 0% -> 0% of each run, Pallas kernels for 2% -> 3%
where the time goes in v3:
time: 72.1 us; the launch traced here: 71 us
  blocking collectives  29.4 us (41%)
  starting transfers between devices  20.6 us (29%)
  waiting for transfers between devices  11.9 us (17%)
  Pallas kernels  8.35 us (12%)
    all_to_all x1, starting transfers between devices, on_device(): kv = exchange(packed, axis_index_groups=[order])  12.2 us
    all_to_all x1, waiting for transfers between devices, on_device(): back = exchange(grads, axis_index_groups=[back_order])  9.26 us
    all_to_all x1, starting transfers between devices, on_device(): back = exchange(grads, axis_index_groups=[back_order])  8.35 us
    pallas_call x7, Pallas kernels, call(): pl.pallas_call(kernel, out_shape=out_shape, in_specs=in_specs, out_specs=...  8.35 us
    all_gather x1, blocking collectives, on_device(): q_all = gather(queries)  8.03 us
    all_gather x1, blocking collectives, on_device(): dq_all = gather(dq)  7.55 us
    all_gather x1, blocking collectives, on_device(): g_all = gather(out_grad)  7.28 us
    all_gather x1, blocking collectives, on_device(): stats_all = gather(stats)  6.52 us
  transfers between devices with their start and end apart: 2, of which 2 were waited for; matrix products, arithmetic and copies ran while one was open for 0% of the time, Pallas kernels for 3%

profile of v3, /device:TPU:7, one launch (start us, length us, event | category | flops | bytes accessed | tf_op | source)
XLA Modules:
  0.0 71.0 jit_solution(13933241742160612914)
XLA Ops:
  0.6 0.0 copy-start.2
  0.6 0.0 copy-start.3
  0.7 0.0 copy-start.1
  0.7 0.0 copy-start
  0.7 2.1 %shard_map.86 = bf16[8,2,208,128]{3,2,1,0:T(8,128)(2,1)} custom-call(bf16[208,1024]{1,0:T(8,128)(2,1)} %keys_ref.1, bf16[208,1024]{1,0:T(8,128)(2,1)} %values_ref.1), custom_call_target="tpu_custom_call" | custom-call | bytes 1703936 | tf_op jit(solution)/shard_map/pallas_call | solution.py:189
  2.8 12.2 %all-to-all-start = ((bf16[8,2,208,128]{3,2,1,0:T(8,128)(2,1)}), bf16[8,2,208,128]{3,2,1,0:T(8,128)(2,1)S(1)}, u32[]{:S(2)}, u32[]{:S(2)}) async-start(bf16[8,2,208,128]{3,2,1,0:T(8,128)(2,1)} %shard_map.86), calls=%async_computation | async-start | bytes 1703936 | tf_op jit(solution)/shard_map/all_to_all | solution.py:230
  15.0 0.0 copy-done.2
  15.0 8.0 %all-gather = bf16[512,512]{1,0:T(8,128)(2,1)S(1)} all-gather(bf16[128,512]{1,0:T(8,128)(2,1)S(1)} %copy-done.2), channel_id=2, replica_groups={{0,8,16,24},{32,40,48,56},{64,72,80,88},{96,104,112,120},{128,136,144,1..., dimensions={0}, use_global_device_ids=true | all-gather | bytes 655360 | tf_op jit(solution)/shard_map/all_gather | solution.py:231
  23.0 0.0 copy-done.3
  23.0 7.3 %all-gather.1 = bf16[512,512]{1,0:T(8,128)(2,1)S(1)} all-gather(bf16[128,512]{1,0:T(8,128)(2,1)S(1)} %copy-done.3), channel_id=3, replica_groups={{0,8,16,24},{32,40,48,56},{64,72,80,88},{96,104,112,120},{128,136,144,1..., dimensions={0}, use_global_device_ids=true | all-gather | bytes 655360 | tf_op jit(solution)/shard_map/all_gather | solution.py:232
  30.3 0.0 copy-done.1
  30.3 0.0 copy-done
  30.3 0.7 shard_map.85
  31.0 2.7 %all-to-all-done.kv_ref = bf16[8,2,208,128]{3,2,1,0:T(8,128)(2,1)S(1)} async-done(((bf16[8,2,208,128]{3,2,1,0:T(8,128)(2,1)}), bf16[8,2,208,128]{3,2,1,0:T(8,128)(2,1)S(1)}, u32[]{:S(2)}, u32[]{:S(2)}) %all-to-all-start) | async-done | bytes 852000 | tf_op jit(solution)/shard_map/all_to_all | solution.py:230
  33.7 1.3 %shard_map.87 = (f32[8,512]{1,0:T(8,128)S(1)}, f32[1664,512]{1,0:T(8,128)S(1)}, f32[1664,512]{1,0:T(8,128)S(1)}) custom-call(bf16[128,512]{1,0:T(8,128)(2,1)S(1)} %get-tuple-element.16.qt_ref, bf16[128,512]{1,0:T(8,128)(2,1)S(1)} %get-tuple-element.17.gt_ref, bf16[8,2,208,128]{3,2,1,0:T(8,128)(2,1)S(1)} %all-to-all-done.kv_ref), custom_call_target="tpu_custom_call" | custom-call | flops 436207616 | bytes 4530176 | tf_op jit(solution)/shard_map/pallas_call | solution.py:189
  35.0 6.5 %all-gather.2 = f32[32,512]{1,0:T(8,128)S(1)} all-gather(f32[8,512]{1,0:T(8,128)S(1)} %get-tuple-element.18.own_ref), channel_id=4, replica_groups={{0,8,16,24},{32,40,48,56},{64,72,80,88},{96,104,112,120},{128,136,144,1..., dimensions={0}, use_global_device_ids=true | all-gather | bytes 81920 | tf_op jit(solution)/shard_map/all_gather | solution.py:259
  41.5 1.9 %shard_map.88 = (bf16[8,2,208,128]{3,2,1,0:T(8,128)(2,1)}, bf16[1664,512]{1,0:T(8,128)(2,1)S(1)}) custom-call(f32[8,512]{1,0:T(8,128)S(1)} %get-tuple-element.15.flag_ref, f32[4,8,512]{2,1,0:T(8,128)S(1)} %bitcast.8, f32[8,512]{1,0:T(8,128)S(1)} %get-tuple-element.18.own_ref, bf16[512,128]{1,0:T(8,128)(2,1)S(1)} %get-tuple-element.19.q_ref, ...), custom_call_target="tpu_custom_call" | custom-call | flops 436207616 | bytes 9732096 | tf_op jit(solution)/shard_map/pallas_call | solution.py:189
  43.4 8.3 %all-to-all-start.1 = ((bf16[8,2,208,128]{3,2,1,0:T(8,128)(2,1)}), bf16[8,2,208,128]{3,2,1,0:T(8,128)(2,1)S(1)}, u32[]{:S(2)}, u32[]{:S(2)}) async-start(bf16[8,2,208,128]{3,2,1,0:T(8,128)(2,1)} %get-tuple-element.24), calls=%async_computation.1 | async-start | bytes 1703936 | tf_op jit(solution)/shard_map/all_to_all | solution.py:269
  51.8 0.6 shard_map.89
  52.4 7.5 %all-gather.3 = bf16[512,512]{1,0:T(8,128)(2,1)S(1)} all-gather(bf16[128,512]{1,0:T(8,128)(2,1)S(1)} %shard_map.89), channel_id=5, replica_groups={{0,8,16,24},{32,40,48,56},{64,72,80,88},{96,104,112,120},{128,136,144,1..., dimensions={0}, use_global_device_ids=true | all-gather | bytes 655360 | tf_op jit(solution)/shard_map/all_gather | solution.py:278
  59.9 0.8 %shard_map.90 = bf16[128,512]{1,0:T(8,128)(2,1)} custom-call(f32[8,512]{1,0:T(8,128)S(1)} %get-tuple-element.15.flag_ref, bf16[4,128,512]{2,1,0:T(8,128)(2,1)S(1)} %bitcast.7), custom_call_target="tpu_custom_call" | custom-call | bytes 671744 | tf_op jit(solution)/shard_map/pallas_call | solution.py:189
  60.7 9.3 %all-to-all-done.1.in_ref = bf16[8,2,208,128]{3,2,1,0:T(8,128)(2,1)S(1)} async-done(((bf16[8,2,208,128]{3,2,1,0:T(8,128)(2,1)}), bf16[8,2,208,128]{3,2,1,0:T(8,128)(2,1)S(1)}, u32[]{:S(2)}, u32[]{:S(2)}) %all-to-all-start.1) | async-done | bytes 852000 | tf_op jit(solution)/shard_map/all_to_all | solution.py:269
  69.9 1.0 %shard_map.91 = (bf16[208,1024]{1,0:T(8,128)(2,1)}, bf16[208,1024]{1,0:T(8,128)(2,1)}) custom-call(bf16[8,2,208,128]{3,2,1,0:T(8,128)(2,1)S(1)} %all-to-all-done.1.in_ref), custom_call_target="tpu_custom_call" | custom-call | bytes 1703936 | tf_op jit(solution)/shard_map/pallas_call | solution.py:189
Async XLA Ops:
  0.6 14.4 %copy-start.2 = (bf16[128,512]{1,0:T(8,128)(2,1)S(1)}, bf16[128,512]{1,0:T(8,128)(2,1)}, u32[]{:S(2)}) copy-start(bf16[128,512]{1,0:T(8,128)(2,1)} %param.6) | copy-start | bytes 393220
  0.6 22.4 %copy-start.3 = (bf16[128,512]{1,0:T(8,128)(2,1)S(1)}, bf16[128,512]{1,0:T(8,128)(2,1)}, u32[]{:S(2)}) copy-start(bf16[128,512]{1,0:T(8,128)(2,1)} %param.9) | copy-start | bytes 393220
  0.7 29.7 %copy-start.1 = (s32[64]{0:T(128)S(1)}, s32[64]{0:T(128)}, u32[]{:S(2)}) copy-start(s32[64]{0:T(128)} %text_ref.1) | copy-start | bytes 772
  0.7 29.7 %copy-start = (s32[64]{0:T(128)S(1)}, s32[64]{0:T(128)}, u32[]{:S(2)}) copy-start(s32[64]{0:T(128)} %counts_ref.1) | copy-start | bytes 772
  2.8 30.9 %all-to-all-start = ((bf16[8,2,208,128]{3,2,1,0:T(8,128)(2,1)}), bf16[8,2,208,128]{3,2,1,0:T(8,128)(2,1)S(1)}, u32[]{:S(2)}, u32[]{:S(2)}) async-start(bf16[8,2,208,128]{3,2,1,0:T(8,128)(2,1)} %shard_map.86), calls=%async_computation | async-start | bytes 1703936 | tf_op jit(solution)/shard_map/all_to_all | solution.py:230
  43.4 26.5 %all-to-all-start.1 = ((bf16[8,2,208,128]{3,2,1,0:T(8,128)(2,1)}), bf16[8,2,208,128]{3,2,1,0:T(8,128)(2,1)S(1)}, u32[]{:S(2)}, u32[]{:S(2)}) async-start(bf16[8,2,208,128]{3,2,1,0:T(8,128)(2,1)} %get-tuple-element.24), calls=%async_computation.1 | async-start | bytes 1703936 | tf_op jit(solution)/shard_map/all_to_all | solution.py:269

commit v4 on v3

--- a/solution.py
+++ b/solution.py
@@ -43,10 +43,6 @@
 def head_rows(block):
     heads = block.shape[1] // HEAD_DIM
     return jnp.concatenate([block[:, h * HEAD_DIM:(h + 1) * HEAD_DIM] for h in range(heads)], axis=0)
-
-
-def member_order(first, size):
-    return [(first + index) % size for index in range(size)]
 
 
 def pack_kernel(order, keys_ref, values_ref, out_ref, held, in_sems, out_sems):
@@ -95,22 +91,27 @@
 def stats_kernel(order, qt_ref, gt_ref, kv_ref, stat_ref, weight_ref, grad_ref):
     parts, rows = kv_ref.shape[0], kv_ref.shape[2]
     q_turned, g_turned = qt_ref[...], gt_ref[...]
+    wide = STEP * rows
     top = None
-    for part in range(parts):
-        scores = jnp.dot(kv_ref[part, 0], q_turned, preferred_element_type=jnp.float32) * SCALE2
-        if (order[part] + 1) * rows > TILE_ROWS:
-            row = lax.broadcasted_iota(jnp.int32, scores.shape, 0) + order[part] * rows
-            scores = jnp.where(row < TILE_ROWS, scores, -1e30)
-        weight_ref[pl.ds(part * rows, rows), :] = scores
+    for part in range(0, parts, STEP):
+        block = kv_ref[part:part + STEP, 0].reshape(wide, HEAD_DIM)
+        scores = jnp.dot(block, q_turned, preferred_element_type=jnp.float32) * SCALE2
+        for place in range(part, part + STEP):
+            dead = (order[place] + 1) * rows - TILE_ROWS
+            if dead > 0:
+                row = lax.broadcasted_iota(jnp.int32, scores.shape, 0) - (place - part) * rows
+                scores = jnp.where((row >= max(rows - dead, 0)) & (row < rows), -1e30, scores)
+        weight_ref[pl.ds(part * rows, wide), :] = scores
         part_top = jnp.max(scores, axis=0, keepdims=True)
         top = part_top if top is None else jnp.maximum(top, part_top)
     total = jnp.zeros_like(top)
     product = jnp.zeros_like(top)
-    for part in range(parts):
-        span = pl.ds(part * rows, rows)
+    for part in range(0, parts, STEP):
+        span = pl.ds(part * rows, wide)
         weights = jnp.exp2(weight_ref[span, :] - top)
         weight_ref[span, :] = weights
-        grads = jnp.dot(kv_ref[part, 1], g_turned, preferred_element_type=jnp.float32)
+        block = kv_ref[part:part + STEP, 1].reshape(wide, HEAD_DIM)
+        grads = jnp.dot(block, g_turned, preferred_element_type=jnp.float32)
         grad_ref[span, :] = grads
         total = total + jnp.sum(weights, axis=0, keepdims=True)
         product = product + jnp.sum(weights * grads, axis=0, keepdims=True)
@@ -181,6 +182,7 @@
 HBM = pl.BlockSpec(memory_space=pltpu.HBM)
 ANY = pl.BlockSpec(memory_space=pl.ANY)
 MIB = 1024 * 1024
+STEP = 4
 
 
 def call(kernel, out_shape, out_specs, in_specs, args, scratch=(), limit=32, flops=0, exps=0):
@@ -201,8 +203,8 @@
     text_rows, width = queries.shape
     rows = keys.shape[0]
     parts = lax.axis_size("tensor")
-    order = member_order(parts - 2, parts)
-    back_order = member_order(parts - 3, parts)
+    order = [7, 3, 2, 4, 1, 5, 0, 6]
+    back_order = [5, 6, 7, 0, 1, 2, 3, 4]
     exchange = functools.partial(lax.all_to_all, axis_name="tensor", split_axis=0, concat_axis=0, tiled=True)
     devices = lax.axis_size("dp")
     groups = [[first + member for member in range(GROUP)] for first in range(0, devices, GROUP)]

time: 72.1 us -> 72.2 us (level)
  blocking collectives: 29.4 us -> 31.4 us
  starting transfers between devices: 20.6 us -> 18.8 us
    all_to_all x1, starting transfers between devices: 8.35 us -> 6.59 us  [on_device(): back = exchange(grads, axis_index_groups=[back_order])]
    all_gather x1, blocking collectives: 6.52 us -> 8.24 us  [on_device(): stats_all = gather(stats)]
where the time goes in v4:
time: 72.2 us; the launch traced here: 70.9 us
  blocking collectives  31.4 us (43%)
  starting transfers between devices  18.8 us (26%)
  waiting for transfers between devices  11.6 us (16%)
  Pallas kernels  8.28 us (11%)
    all_to_all x1, starting transfers between devices, on_device(): kv = exchange(packed, axis_index_groups=[order])  12.3 us
    all_to_all x1, waiting for transfers between devices, on_device(): back = exchange(grads, axis_index_groups=[back_order])  8.63 us
    pallas_call x7, Pallas kernels, call(): pl.pallas_call(kernel, out_shape=out_shape, in_specs=in_specs, out_specs=...  8.28 us
    all_gather x1, blocking collectives, on_device(): stats_all = gather(stats)  8.24 us
    all_gather x1, blocking collectives, on_device(): q_all = gather(queries)  8.03 us
    all_gather x1, blocking collectives, on_device(): dq_all = gather(dq)  7.83 us
    all_gather x1, blocking collectives, on_device(): g_all = gather(out_grad)  7.28 us
    all_to_all x1, starting transfers between devices, on_device(): back = exchange(grads, axis_index_groups=[back_order])  6.59 us
  transfers between devices with their start and end apart: 2, of which 2 were waited for; matrix products, arithmetic and copies ran while one was open for 0% of the time, Pallas kernels for 3%

profile of v4, /device:TPU:7, one launch (start us, length us, event | category | flops | bytes accessed | tf_op | source)
XLA Modules:
  0.0 70.9 jit_solution(4906231978127622813)
XLA Ops:
  0.6 0.0 copy-start.2
  0.6 0.0 copy-start.3
  0.7 0.0 copy-start.1
  0.7 0.0 copy-start
  0.7 2.1 %shard_map.86 = bf16[8,2,208,128]{3,2,1,0:T(8,128)(2,1)} custom-call(bf16[208,1024]{1,0:T(8,128)(2,1)} %keys_ref.1, bf16[208,1024]{1,0:T(8,128)(2,1)} %values_ref.1), custom_call_target="tpu_custom_call" | custom-call | bytes 1703936 | tf_op jit(solution)/shard_map/pallas_call | solution.py:191
  2.8 12.3 %all-to-all-start = ((bf16[8,2,208,128]{3,2,1,0:T(8,128)(2,1)}), bf16[8,2,208,128]{3,2,1,0:T(8,128)(2,1)S(1)}, u32[]{:S(2)}, u32[]{:S(2)}) async-start(bf16[8,2,208,128]{3,2,1,0:T(8,128)(2,1)} %shard_map.86), calls=%async_computation | async-start | bytes 1703936 | tf_op jit(solution)/shard_map/all_to_all | solution.py:232
  15.0 0.0 copy-done.2
  15.0 8.0 %all-gather = bf16[512,512]{1,0:T(8,128)(2,1)S(1)} all-gather(bf16[128,512]{1,0:T(8,128)(2,1)S(1)} %copy-done.2), channel_id=2, replica_groups={{0,8,16,24},{32,40,48,56},{64,72,80,88},{96,104,112,120},{128,136,144,1..., dimensions={0}, use_global_device_ids=true | all-gather | bytes 655360 | tf_op jit(solution)/shard_map/all_gather | solution.py:233
  23.1 0.0 copy-done.3
  23.1 7.3 %all-gather.1 = bf16[512,512]{1,0:T(8,128)(2,1)S(1)} all-gather(bf16[128,512]{1,0:T(8,128)(2,1)S(1)} %copy-done.3), channel_id=3, replica_groups={{0,8,16,24},{32,40,48,56},{64,72,80,88},{96,104,112,120},{128,136,144,1..., dimensions={0}, use_global_device_ids=true | all-gather | bytes 655360 | tf_op jit(solution)/shard_map/all_gather | solution.py:234
  30.4 0.0 copy-done.1
  30.4 0.0 copy-done
  30.4 0.7 shard_map.85
  31.1 3.0 %all-to-all-done.kv_ref = bf16[8,2,208,128]{3,2,1,0:T(8,128)(2,1)S(1)} async-done(((bf16[8,2,208,128]{3,2,1,0:T(8,128)(2,1)}), bf16[8,2,208,128]{3,2,1,0:T(8,128)(2,1)S(1)}, u32[]{:S(2)}, u32[]{:S(2)}) %all-to-all-start) | async-done | bytes 852000 | tf_op jit(solution)/shard_map/all_to_all | solution.py:232
  34.1 1.2 %shard_map.87 = (f32[8,512]{1,0:T(8,128)S(1)}, f32[1664,512]{1,0:T(8,128)S(1)}, f32[1664,512]{1,0:T(8,128)S(1)}) custom-call(bf16[128,512]{1,0:T(8,128)(2,1)S(1)} %get-tuple-element.16.qt_ref, bf16[128,512]{1,0:T(8,128)(2,1)S(1)} %get-tuple-element.17.gt_ref, bf16[8,2,208,128]{3,2,1,0:T(8,128)(2,1)S(1)} %all-to-all-done.kv_ref), custom_call_target="tpu_custom_call" | custom-call | flops 436207616 | bytes 4530176 | tf_op jit(solution)/shard_map/pallas_call | solution.py:191
  35.3 8.2 %all-gather.2 = f32[32,512]{1,0:T(8,128)S(1)} all-gather(f32[8,512]{1,0:T(8,128)S(1)} %get-tuple-element.18.own_ref), channel_id=4, replica_groups={{0,8,16,24},{32,40,48,56},{64,72,80,88},{96,104,112,120},{128,136,144,1..., dimensions={0}, use_global_device_ids=true | all-gather | bytes 81920 | tf_op jit(solution)/shard_map/all_gather | solution.py:261
  43.6 1.9 %shard_map.88 = (bf16[8,2,208,128]{3,2,1,0:T(8,128)(2,1)}, bf16[1664,512]{1,0:T(8,128)(2,1)S(1)}) custom-call(f32[8,512]{1,0:T(8,128)S(1)} %get-tuple-element.15.flag_ref, f32[4,8,512]{2,1,0:T(8,128)S(1)} %bitcast.8, f32[8,512]{1,0:T(8,128)S(1)} %get-tuple-element.18.own_ref, bf16[512,128]{1,0:T(8,128)(2,1)S(1)} %get-tuple-element.19.q_ref, ...), custom_call_target="tpu_custom_call" | custom-call | flops 436207616 | bytes 9732096 | tf_op jit(solution)/shard_map/pallas_call | solution.py:191
  45.5 6.6 %all-to-all-start.1 = ((bf16[8,2,208,128]{3,2,1,0:T(8,128)(2,1)}), bf16[8,2,208,128]{3,2,1,0:T(8,128)(2,1)S(1)}, u32[]{:S(2)}, u32[]{:S(2)}) async-start(bf16[8,2,208,128]{3,2,1,0:T(8,128)(2,1)} %get-tuple-element.24), calls=%async_computation.1 | async-start | bytes 1703936 | tf_op jit(solution)/shard_map/all_to_all | solution.py:271
  52.0 0.6 shard_map.89
  52.6 7.8 %all-gather.3 = bf16[512,512]{1,0:T(8,128)(2,1)S(1)} all-gather(bf16[128,512]{1,0:T(8,128)(2,1)S(1)} %shard_map.89), channel_id=5, replica_groups={{0,8,16,24},{32,40,48,56},{64,72,80,88},{96,104,112,120},{128,136,144,1..., dimensions={0}, use_global_device_ids=true | all-gather | bytes 655360 | tf_op jit(solution)/shard_map/all_gather | solution.py:280
  60.5 0.8 %shard_map.90 = bf16[128,512]{1,0:T(8,128)(2,1)} custom-call(f32[8,512]{1,0:T(8,128)S(1)} %get-tuple-element.15.flag_ref, bf16[4,128,512]{2,1,0:T(8,128)(2,1)S(1)} %bitcast.7), custom_call_target="tpu_custom_call" | custom-call | bytes 671744 | tf_op jit(solution)/shard_map/pallas_call | solution.py:191
  61.2 8.6 %all-to-all-done.1.in_ref = bf16[8,2,208,128]{3,2,1,0:T(8,128)(2,1)S(1)} async-done(((bf16[8,2,208,128]{3,2,1,0:T(8,128)(2,1)}), bf16[8,2,208,128]{3,2,1,0:T(8,128)(2,1)S(1)}, u32[]{:S(2)}, u32[]{:S(2)}) %all-to-all-start.1) | async-done | bytes 852000 | tf_op jit(solution)/shard_map/all_to_all | solution.py:271
  69.8 1.0 %shard_map.91 = (bf16[208,1024]{1,0:T(8,128)(2,1)}, bf16[208,1024]{1,0:T(8,128)(2,1)}) custom-call(bf16[8,2,208,128]{3,2,1,0:T(8,128)(2,1)S(1)} %all-to-all-done.1.in_ref), custom_call_target="tpu_custom_call" | custom-call | bytes 1703936 | tf_op jit(solution)/shard_map/pallas_call | solution.py:191
Async XLA Ops:
  0.6 14.4 %copy-start.2 = (bf16[128,512]{1,0:T(8,128)(2,1)S(1)}, bf16[128,512]{1,0:T(8,128)(2,1)}, u32[]{:S(2)}) copy-start(bf16[128,512]{1,0:T(8,128)(2,1)} %param.6) | copy-start | bytes 393220
  0.6 22.4 %copy-start.3 = (bf16[128,512]{1,0:T(8,128)(2,1)S(1)}, bf16[128,512]{1,0:T(8,128)(2,1)}, u32[]{:S(2)}) copy-start(bf16[128,512]{1,0:T(8,128)(2,1)} %param.9) | copy-start | bytes 393220
  0.7 29.7 %copy-start.1 = (s32[64]{0:T(128)S(1)}, s32[64]{0:T(128)}, u32[]{:S(2)}) copy-start(s32[64]{0:T(128)} %text_ref.1) | copy-start | bytes 772
  0.7 29.7 %copy-start = (s32[64]{0:T(128)S(1)}, s32[64]{0:T(128)}, u32[]{:S(2)}) copy-start(s32[64]{0:T(128)} %counts_ref.1) | copy-start | bytes 772
  2.8 31.3 %all-to-all-start = ((bf16[8,2,208,128]{3,2,1,0:T(8,128)(2,1)}), bf16[8,2,208,128]{3,2,1,0:T(8,128)(2,1)S(1)}, u32[]{:S(2)}, u32[]{:S(2)}) async-start(bf16[8,2,208,128]{3,2,1,0:T(8,128)(2,1)} %shard_map.86), calls=%async_computation | async-start | bytes 1703936 | tf_op jit(solution)/shard_map/all_to_all | solution.py:232
  45.5 24.4 %all-to-all-start.1 = ((bf16[8,2,208,128]{3,2,1,0:T(8,128)(2,1)}), bf16[8,2,208,128]{3,2,1,0:T(8,128)(2,1)S(1)}, u32[]{:S(2)}, u32[]{:S(2)}) async-start(bf16[8,2,208,128]{3,2,1,0:T(8,128)(2,1)} %get-tuple-element.24), calls=%async_computation.1 | async-start | bytes 1703936 | tf_op jit(solution)/shard_map/all_to_all | solution.py:271

commit v5 on v3

--- a/solution.py
+++ b/solution.py
@@ -45,10 +45,6 @@
     return jnp.concatenate([block[:, h * HEAD_DIM:(h + 1) * HEAD_DIM] for h in range(heads)], axis=0)
 
 
-def member_order(first, size):
-    return [(first + index) % size for index in range(size)]
-
-
 def pack_kernel(order, keys_ref, values_ref, out_ref, held, in_sems, out_sems):
     parts = out_ref.shape[0]
     loads = []
@@ -201,8 +197,8 @@
     text_rows, width = queries.shape
     rows = keys.shape[0]
     parts = lax.axis_size("tensor")
-    order = member_order(parts - 2, parts)
-    back_order = member_order(parts - 3, parts)
+    order = [7, 3, 2, 4, 1, 5, 0, 6]
+    back_order = [5, 6, 7, 0, 1, 2, 3, 4]
     exchange = functools.partial(lax.all_to_all, axis_name="tensor", split_axis=0, concat_axis=0, tiled=True)
     devices = lax.axis_size("dp")
     groups = [[first + member for member in range(GROUP)] for first in range(0, devices, GROUP)]

time: 72.1 us -> 72.3 us (level)
  blocking collectives: 29.4 us -> 31.4 us
  starting transfers between devices: 20.6 us -> 18.8 us
    all_to_all x1, starting transfers between devices: 8.35 us -> 6.59 us  [on_device(): back = exchange(grads, axis_index_groups=[back_order])]
    all_gather x1, blocking collectives: 6.52 us -> 8.24 us  [on_device(): stats_all = gather(stats)]
where the time goes in v5:
time: 72.3 us; the launch traced here: 71 us
  blocking collectives  31.4 us (43%)
  starting transfers between devices  18.8 us (26%)
  waiting for transfers between devices  11.6 us (16%)
  Pallas kernels  8.37 us (12%)
    all_to_all x1, starting transfers between devices, on_device(): kv = exchange(packed, axis_index_groups=[order])  12.3 us
    all_to_all x1, waiting for transfers between devices, on_device(): back = exchange(grads, axis_index_groups=[back_order])  8.62 us
    pallas_call x7, Pallas kernels, call(): pl.pallas_call(kernel, out_shape=out_shape, in_specs=in_specs, out_specs=...  8.37 us
    all_gather x1, blocking collectives, on_device(): stats_all = gather(stats)  8.24 us
    all_gather x1, blocking collectives, on_device(): q_all = gather(queries)  8.03 us
    all_gather x1, blocking collectives, on_device(): dq_all = gather(dq)  7.83 us
    all_gather x1, blocking collectives, on_device(): g_all = gather(out_grad)  7.28 us
    all_to_all x1, starting transfers between devices, on_device(): back = exchange(grads, axis_index_groups=[back_order])  6.59 us
  transfers between devices with their start and end apart: 2, of which 2 were waited for; matrix products, arithmetic and copies ran while one was open for 0% of the time, Pallas kernels for 3%

profile of v5, /device:TPU:7, one launch (start us, length us, event | category | flops | bytes accessed | tf_op | source)
XLA Modules:
  0.0 71.0 jit_solution(487013341315197101)
XLA Ops:
  0.6 0.0 copy-start.2
  0.6 0.0 copy-start.3
  0.7 0.0 copy-start.1
  0.7 0.0 copy-start
  0.7 2.1 %shard_map.86 = bf16[8,2,208,128]{3,2,1,0:T(8,128)(2,1)} custom-call(bf16[208,1024]{1,0:T(8,128)(2,1)} %keys_ref.1, bf16[208,1024]{1,0:T(8,128)(2,1)} %values_ref.1), custom_call_target="tpu_custom_call" | custom-call | bytes 1703936 | tf_op jit(solution)/shard_map/pallas_call | solution.py:185
  2.8 12.3 %all-to-all-start = ((bf16[8,2,208,128]{3,2,1,0:T(8,128)(2,1)}), bf16[8,2,208,128]{3,2,1,0:T(8,128)(2,1)S(1)}, u32[]{:S(2)}, u32[]{:S(2)}) async-start(bf16[8,2,208,128]{3,2,1,0:T(8,128)(2,1)} %shard_map.86), calls=%async_computation | async-start | bytes 1703936 | tf_op jit(solution)/shard_map/all_to_all | solution.py:226
  15.0 0.0 copy-done.2
  15.0 8.0 %all-gather = bf16[512,512]{1,0:T(8,128)(2,1)S(1)} all-gather(bf16[128,512]{1,0:T(8,128)(2,1)S(1)} %copy-done.2), channel_id=2, replica_groups={{0,8,16,24},{32,40,48,56},{64,72,80,88},{96,104,112,120},{128,136,144,1..., dimensions={0}, use_global_device_ids=true | all-gather | bytes 655360 | tf_op jit(solution)/shard_map/all_gather | solution.py:227
  23.1 0.0 copy-done.3
  23.1 7.3 %all-gather.1 = bf16[512,512]{1,0:T(8,128)(2,1)S(1)} all-gather(bf16[128,512]{1,0:T(8,128)(2,1)S(1)} %copy-done.3), channel_id=3, replica_groups={{0,8,16,24},{32,40,48,56},{64,72,80,88},{96,104,112,120},{128,136,144,1..., dimensions={0}, use_global_device_ids=true | all-gather | bytes 655360 | tf_op jit(solution)/shard_map/all_gather | solution.py:228
  30.4 0.0 copy-done.1
  30.4 0.0 copy-done
  30.4 0.7 shard_map.85
  31.1 3.0 %all-to-all-done.kv_ref = bf16[8,2,208,128]{3,2,1,0:T(8,128)(2,1)S(1)} async-done(((bf16[8,2,208,128]{3,2,1,0:T(8,128)(2,1)}), bf16[8,2,208,128]{3,2,1,0:T(8,128)(2,1)S(1)}, u32[]{:S(2)}, u32[]{:S(2)}) %all-to-all-start) | async-done | bytes 852000 | tf_op jit(solution)/shard_map/all_to_all | solution.py:226
  34.1 1.3 %shard_map.87 = (f32[8,512]{1,0:T(8,128)S(1)}, f32[1664,512]{1,0:T(8,128)S(1)}, f32[1664,512]{1,0:T(8,128)S(1)}) custom-call(bf16[128,512]{1,0:T(8,128)(2,1)S(1)} %get-tuple-element.16.qt_ref, bf16[128,512]{1,0:T(8,128)(2,1)S(1)} %get-tuple-element.17.gt_ref, bf16[8,2,208,128]{3,2,1,0:T(8,128)(2,1)S(1)} %all-to-all-done.kv_ref), custom_call_target="tpu_custom_call" | custom-call | flops 436207616 | bytes 4530176 | tf_op jit(solution)/shard_map/pallas_call | solution.py:185
  35.4 8.2 %all-gather.2 = f32[32,512]{1,0:T(8,128)S(1)} all-gather(f32[8,512]{1,0:T(8,128)S(1)} %get-tuple-element.18.own_ref), channel_id=4, replica_groups={{0,8,16,24},{32,40,48,56},{64,72,80,88},{96,104,112,120},{128,136,144,1..., dimensions={0}, use_global_device_ids=true | all-gather | bytes 81920 | tf_op jit(solution)/shard_map/all_gather | solution.py:255
  43.6 1.9 %shard_map.88 = (bf16[8,2,208,128]{3,2,1,0:T(8,128)(2,1)}, bf16[1664,512]{1,0:T(8,128)(2,1)S(1)}) custom-call(f32[8,512]{1,0:T(8,128)S(1)} %get-tuple-element.15.flag_ref, f32[4,8,512]{2,1,0:T(8,128)S(1)} %bitcast.8, f32[8,512]{1,0:T(8,128)S(1)} %get-tuple-element.18.own_ref, bf16[512,128]{1,0:T(8,128)(2,1)S(1)} %get-tuple-element.19.q_ref, ...), custom_call_target="tpu_custom_call" | custom-call | flops 436207616 | bytes 9732096 | tf_op jit(solution)/shard_map/pallas_call | solution.py:185
  45.5 6.6 %all-to-all-start.1 = ((bf16[8,2,208,128]{3,2,1,0:T(8,128)(2,1)}), bf16[8,2,208,128]{3,2,1,0:T(8,128)(2,1)S(1)}, u32[]{:S(2)}, u32[]{:S(2)}) async-start(bf16[8,2,208,128]{3,2,1,0:T(8,128)(2,1)} %get-tuple-element.24), calls=%async_computation.1 | async-start | bytes 1703936 | tf_op jit(solution)/shard_map/all_to_all | solution.py:265
  52.1 0.6 shard_map.89
  52.7 7.8 %all-gather.3 = bf16[512,512]{1,0:T(8,128)(2,1)S(1)} all-gather(bf16[128,512]{1,0:T(8,128)(2,1)S(1)} %shard_map.89), channel_id=5, replica_groups={{0,8,16,24},{32,40,48,56},{64,72,80,88},{96,104,112,120},{128,136,144,1..., dimensions={0}, use_global_device_ids=true | all-gather | bytes 655360 | tf_op jit(solution)/shard_map/all_gather | solution.py:274
  60.5 0.8 %shard_map.90 = bf16[128,512]{1,0:T(8,128)(2,1)} custom-call(f32[8,512]{1,0:T(8,128)S(1)} %get-tuple-element.15.flag_ref, bf16[4,128,512]{2,1,0:T(8,128)(2,1)S(1)} %bitcast.7), custom_call_target="tpu_custom_call" | custom-call | bytes 671744 | tf_op jit(solution)/shard_map/pallas_call | solution.py:185
  61.3 8.6 %all-to-all-done.1.in_ref = bf16[8,2,208,128]{3,2,1,0:T(8,128)(2,1)S(1)} async-done(((bf16[8,2,208,128]{3,2,1,0:T(8,128)(2,1)}), bf16[8,2,208,128]{3,2,1,0:T(8,128)(2,1)S(1)}, u32[]{:S(2)}, u32[]{:S(2)}) %all-to-all-start.1) | async-done | bytes 852000 | tf_op jit(solution)/shard_map/all_to_all | solution.py:265
  69.9 1.0 %shard_map.91 = (bf16[208,1024]{1,0:T(8,128)(2,1)}, bf16[208,1024]{1,0:T(8,128)(2,1)}) custom-call(bf16[8,2,208,128]{3,2,1,0:T(8,128)(2,1)S(1)} %all-to-all-done.1.in_ref), custom_call_target="tpu_custom_call" | custom-call | bytes 1703936 | tf_op jit(solution)/shard_map/pallas_call | solution.py:185
Async XLA Ops:
  0.6 14.4 %copy-start.2 = (bf16[128,512]{1,0:T(8,128)(2,1)S(1)}, bf16[128,512]{1,0:T(8,128)(2,1)}, u32[]{:S(2)}) copy-start(bf16[128,512]{1,0:T(8,128)(2,1)} %param.6) | copy-start | bytes 393220
  0.6 22.4 %copy-start.3 = (bf16[128,512]{1,0:T(8,128)(2,1)S(1)}, bf16[128,512]{1,0:T(8,128)(2,1)}, u32[]{:S(2)}) copy-start(bf16[128,512]{1,0:T(8,128)(2,1)} %param.9) | copy-start | bytes 393220
  0.7 29.7 %copy-start.1 = (s32[64]{0:T(128)S(1)}, s32[64]{0:T(128)}, u32[]{:S(2)}) copy-start(s32[64]{0:T(128)} %text_ref.1) | copy-start | bytes 772
  0.7 29.7 %copy-start = (s32[64]{0:T(128)S(1)}, s32[64]{0:T(128)}, u32[]{:S(2)}) copy-start(s32[64]{0:T(128)} %counts_ref.1) | copy-start | bytes 772
  2.8 31.3 %all-to-all-start = ((bf16[8,2,208,128]{3,2,1,0:T(8,128)(2,1)}), bf16[8,2,208,128]{3,2,1,0:T(8,128)(2,1)S(1)}, u32[]{:S(2)}, u32[]{:S(2)}) async-start(bf16[8,2,208,128]{3,2,1,0:T(8,128)(2,1)} %shard_map.86), calls=%async_computation | async-start | bytes 1703936 | tf_op jit(solution)/shard_map/all_to_all | solution.py:226
  45.5 24.4 %all-to-all-start.1 = ((bf16[8,2,208,128]{3,2,1,0:T(8,128)(2,1)}), bf16[8,2,208,128]{3,2,1,0:T(8,128)(2,1)S(1)}, u32[]{:S(2)}, u32[]{:S(2)}) async-start(bf16[8,2,208,128]{3,2,1,0:T(8,128)(2,1)} %get-tuple-element.24), calls=%async_computation.1 | async-start | bytes 1703936 | tf_op jit(solution)/shard_map/all_to_all | solution.py:265

commit v6 on v5

--- a/solution.py
+++ b/solution.py
@@ -45,12 +45,21 @@
     return jnp.concatenate([block[:, h * HEAD_DIM:(h + 1) * HEAD_DIM] for h in range(heads)], axis=0)
 
 
+def member_orders(size):
+    return ([7, 1, 3, 5, 6, 0, 2, 4], [7, 0, 1, 2, 3, 4, 5, 6])
+
+
+def column(orders, part):
+    core = lax.axis_index("dp") % 2
+    return pl.multiple_of(jnp.where(core == 0, orders[0][part], orders[1][part]) * HEAD_DIM, HEAD_DIM)
+
+
 def pack_kernel(order, keys_ref, values_ref, out_ref, held, in_sems, out_sems):
     parts = out_ref.shape[0]
     loads = []
     for part in range(parts):
         for side, ref in enumerate((keys_ref, values_ref)):
-            columns = ref.at[:, pl.ds(order[part] * HEAD_DIM, HEAD_DIM)]
+            columns = ref.at[:, pl.ds(column(order, part), HEAD_DIM)]
             loads.append(pltpu.make_async_copy(columns, held.at[part, side], in_sems.at[part, side]))
             loads[-1].start()
     stores = []
@@ -67,7 +76,7 @@
     copies = []
     for side, ref in enumerate((keys_ref, values_ref)):
         for part in range(in_ref.shape[0]):
-            columns = ref.at[:, pl.ds(order[part] * HEAD_DIM, HEAD_DIM)]
+            columns = ref.at[:, pl.ds(column(order, part), HEAD_DIM)]
             copies.append(pltpu.make_async_copy(in_ref.at[part, side], columns, sems.at[part, side]))
     for copy in copies:
         copy.start()
@@ -197,10 +206,17 @@
     text_rows, width = queries.shape
     rows = keys.shape[0]
     parts = lax.axis_size("tensor")
-    order = [7, 3, 2, 4, 1, 5, 0, 6]
-    back_order = [5, 6, 7, 0, 1, 2, 3, 4]
-    exchange = functools.partial(lax.all_to_all, axis_name="tensor", split_axis=0, concat_axis=0, tiled=True)
     devices = lax.axis_size("dp")
+    orders = member_orders(parts)
+    members = [[dp * parts + member for member in orders[dp % 2]] for dp in range(devices)]
+    exchange = functools.partial(
+        lax.all_to_all,
+        axis_name=("dp", "tensor"),
+        split_axis=0,
+        concat_axis=0,
+        axis_index_groups=members,
+        tiled=True,
+    )
     groups = [[first + member for member in range(GROUP)] for first in range(0, devices, GROUP)]
     gather = functools.partial(lax.all_gather, axis_name="dp", axis_index_groups=groups)
     position = lax.axis_index("dp").astype(jnp.int32).reshape(1)
@@ -211,7 +227,7 @@
     blocks = (parts, 2, rows, HEAD_DIM)
 
     packed = call(
-        functools.partial(pack_kernel, order),
+        functools.partial(pack_kernel, orders),
         pltpu.HBM(blocks, half),
         HBM,
         [ANY, ANY],
@@ -223,7 +239,7 @@
         ],
         limit=60,
     )
-    kv = exchange(packed, axis_index_groups=[order])
+    kv = exchange(packed)
     q_all = gather(queries)
     g_all = gather(out_grad)
     flags, q_turned, g_turned, q_rows, g_rows = call(
@@ -240,7 +256,7 @@
         (position, tile_counts, text_sample, q_all, g_all),
     )
     stats, weights, grad_prod = call(
-        functools.partial(stats_kernel, order),
+        functools.partial(stats_kernel, orders[0]),
         (
             pltpu.VMEM((8, heads), full),
             pltpu.VMEM((parts * rows, heads), full),
@@ -254,7 +270,7 @@
     )
     stats_all = gather(stats)
     grads, dscore = call(
-        functools.partial(grads_kernel, [back_order.index(member) for member in order]),
+        functools.partial(grads_kernel, list(range(parts))),
         (pltpu.HBM(blocks, half), pltpu.VMEM((parts * rows, heads), half)),
         (HBM, VMEM),
         [VMEM] * 7,
@@ -262,7 +278,7 @@
         scratch=[pltpu.VMEM(blocks, half), pltpu.SemaphoreType.DMA((parts,))],
         flops=2 * matmul,
     )
-    back = exchange(grads, axis_index_groups=[back_order])
+    back = exchange(grads)
     dq = call(
         text_grad_kernel,
         pltpu.VMEM((text_rows, width), half),
@@ -277,7 +293,7 @@
     )
     tile = jax.ShapeDtypeStruct((rows, parts * HEAD_DIM), half)
     key_grad, value_grad = call(
-        functools.partial(unpack_kernel, back_order),
+        functools.partial(unpack_kernel, orders),
         (tile, tile),
         (ANY, ANY),
         [ANY],

time: 72.3 us -> 72.3 us (level)
  waiting for transfers between devices: 11.6 us -> 13.8 us
  blocking collectives: 31.4 us -> 30 us
  starting transfers between devices: 18.8 us -> 18 us
    all_to_all x2, waiting for transfers between devices: 11.6 us -> 13.8 us  [the longest x1 10.3 us: on_device(): back = exchange(grads)]
    all_gather x1, blocking collectives: 8.24 us -> 6.86 us  [on_device(): stats_all = gather(stats)]
    all_to_all x2, starting transfers between devices: 18.8 us -> 18 us  [the longest x1 12.2 us: on_device(): kv = exchange(packed)]
where the time goes in v6:
time: 72.3 us; the launch traced here: 70.9 us
  blocking collectives  30 us (41%)
  starting transfers between devices  18 us (25%)
  waiting for transfers between devices  13.8 us (19%)
  Pallas kernels  8.36 us (12%)
    all_to_all x1, starting transfers between devices, on_device(): kv = exchange(packed)  12.2 us
    all_to_all x1, waiting for transfers between devices, on_device(): back = exchange(grads)  10.3 us
    pallas_call x7, Pallas kernels, call(): pl.pallas_call(kernel, out_shape=out_shape, in_specs=in_specs, out_specs=...  8.36 us
    all_gather x1, blocking collectives, on_device(): q_all = gather(queries)  8.06 us
    all_gather x1, blocking collectives, on_device(): dq_all = gather(dq)  7.84 us
    all_gather x1, blocking collectives, on_device(): g_all = gather(out_grad)  7.28 us
    all_gather x1, blocking collectives, on_device(): stats_all = gather(stats)  6.86 us
    all_to_all x1, starting transfers between devices, on_device(): back = exchange(grads)  5.77 us
  transfers between devices with their start and end apart: 2, of which 2 were waited for; matrix products, arithmetic and copies ran while one was open for 0% of the time, Pallas kernels for 3%

profile of v6, /device:TPU:7, one launch (start us, length us, event | category | flops | bytes accessed | tf_op | source)
XLA Modules:
  0.0 70.9 jit_solution(10463474758625461032)
XLA Ops:
  0.6 0.0 copy-start.2
  0.6 0.0 copy-start.3
  0.7 0.0 copy-start.1
  0.7 0.0 copy-start
  0.7 2.1 %shard_map.86 = bf16[8,2,208,128]{3,2,1,0:T(8,128)(2,1)} custom-call(bf16[208,1024]{1,0:T(8,128)(2,1)} %keys_ref.1, bf16[208,1024]{1,0:T(8,128)(2,1)} %values_ref.1), custom_call_target="tpu_custom_call" | custom-call | bytes 1703936 | tf_op jit(solution)/shard_map/pallas_call | solution.py:194
  2.8 12.2 %all-to-all-start = ((bf16[8,2,208,128]{3,2,1,0:T(8,128)(2,1)}), bf16[8,2,208,128]{3,2,1,0:T(8,128)(2,1)S(1)}, u32[]{:S(2)}, u32[]{:S(2)}) async-start(bf16[8,2,208,128]{3,2,1,0:T(8,128)(2,1)} %shard_map.86), calls=%async_computation | async-start | bytes 1703936 | tf_op jit(solution)/shard_map/all_to_all | solution.py:242
  15.0 0.0 copy-done.2
  15.0 8.1 %all-gather = bf16[512,512]{1,0:T(8,128)(2,1)S(1)} all-gather(bf16[128,512]{1,0:T(8,128)(2,1)S(1)} %copy-done.2), channel_id=2, replica_groups={{0,8,16,24},{32,40,48,56},{64,72,80,88},{96,104,112,120},{128,136,144,1..., dimensions={0}, use_global_device_ids=true | all-gather | bytes 655360 | tf_op jit(solution)/shard_map/all_gather | solution.py:243
  23.1 0.0 copy-done.3
  23.1 7.3 %all-gather.1 = bf16[512,512]{1,0:T(8,128)(2,1)S(1)} all-gather(bf16[128,512]{1,0:T(8,128)(2,1)S(1)} %copy-done.3), channel_id=3, replica_groups={{0,8,16,24},{32,40,48,56},{64,72,80,88},{96,104,112,120},{128,136,144,1..., dimensions={0}, use_global_device_ids=true | all-gather | bytes 655360 | tf_op jit(solution)/shard_map/all_gather | solution.py:244
  30.4 0.0 copy-done.1
  30.4 0.0 copy-done
  30.4 0.7 shard_map.85
  31.1 3.4 %all-to-all-done.kv_ref = bf16[8,2,208,128]{3,2,1,0:T(8,128)(2,1)S(1)} async-done(((bf16[8,2,208,128]{3,2,1,0:T(8,128)(2,1)}), bf16[8,2,208,128]{3,2,1,0:T(8,128)(2,1)S(1)}, u32[]{:S(2)}, u32[]{:S(2)}) %all-to-all-start) | async-done | bytes 852000 | tf_op jit(solution)/shard_map/all_to_all | solution.py:242
  34.5 1.3 %shard_map.87 = (f32[8,512]{1,0:T(8,128)S(1)}, f32[1664,512]{1,0:T(8,128)S(1)}, f32[1664,512]{1,0:T(8,128)S(1)}) custom-call(bf16[128,512]{1,0:T(8,128)(2,1)S(1)} %get-tuple-element.16.qt_ref, bf16[128,512]{1,0:T(8,128)(2,1)S(1)} %get-tuple-element.17.gt_ref, bf16[8,2,208,128]{3,2,1,0:T(8,128)(2,1)S(1)} %all-to-all-done.kv_ref), custom_call_target="tpu_custom_call" | custom-call | flops 436207616 | bytes 4530176 | tf_op jit(solution)/shard_map/pallas_call | solution.py:194
  35.8 6.9 %all-gather.2 = f32[32,512]{1,0:T(8,128)S(1)} all-gather(f32[8,512]{1,0:T(8,128)S(1)} %get-tuple-element.18.own_ref), channel_id=4, replica_groups={{0,8,16,24},{32,40,48,56},{64,72,80,88},{96,104,112,120},{128,136,144,1..., dimensions={0}, use_global_device_ids=true | all-gather | bytes 81920 | tf_op jit(solution)/shard_map/all_gather | solution.py:271
  42.7 1.9 %shard_map.88 = (bf16[8,2,208,128]{3,2,1,0:T(8,128)(2,1)}, bf16[1664,512]{1,0:T(8,128)(2,1)S(1)}) custom-call(f32[8,512]{1,0:T(8,128)S(1)} %get-tuple-element.15.flag_ref, f32[4,8,512]{2,1,0:T(8,128)S(1)} %bitcast.8, f32[8,512]{1,0:T(8,128)S(1)} %get-tuple-element.18.own_ref, bf16[512,128]{1,0:T(8,128)(2,1)S(1)} %get-tuple-element.19.q_ref, ...), custom_call_target="tpu_custom_call" | custom-call | flops 436207616 | bytes 9732096 | tf_op jit(solution)/shard_map/pallas_call | solution.py:194
  44.6 5.8 %all-to-all-start.1 = ((bf16[8,2,208,128]{3,2,1,0:T(8,128)(2,1)}), bf16[8,2,208,128]{3,2,1,0:T(8,128)(2,1)S(1)}, u32[]{:S(2)}, u32[]{:S(2)}) async-start(bf16[8,2,208,128]{3,2,1,0:T(8,128)(2,1)} %get-tuple-element.24), calls=%async_computation.1 | async-start | bytes 1703936 | tf_op jit(solution)/shard_map/all_to_all | solution.py:281
  50.4 0.6 shard_map.89
  50.9 7.8 %all-gather.3 = bf16[512,512]{1,0:T(8,128)(2,1)S(1)} all-gather(bf16[128,512]{1,0:T(8,128)(2,1)S(1)} %shard_map.89), channel_id=5, replica_groups={{0,8,16,24},{32,40,48,56},{64,72,80,88},{96,104,112,120},{128,136,144,1..., dimensions={0}, use_global_device_ids=true | all-gather | bytes 655360 | tf_op jit(solution)/shard_map/all_gather | solution.py:290
  58.8 0.8 %shard_map.90 = bf16[128,512]{1,0:T(8,128)(2,1)} custom-call(f32[8,512]{1,0:T(8,128)S(1)} %get-tuple-element.15.flag_ref, bf16[4,128,512]{2,1,0:T(8,128)(2,1)S(1)} %bitcast.7), custom_call_target="tpu_custom_call" | custom-call | bytes 671744 | tf_op jit(solution)/shard_map/pallas_call | solution.py:194
  59.5 10.3 %all-to-all-done.1.in_ref = bf16[8,2,208,128]{3,2,1,0:T(8,128)(2,1)S(1)} async-done(((bf16[8,2,208,128]{3,2,1,0:T(8,128)(2,1)}), bf16[8,2,208,128]{3,2,1,0:T(8,128)(2,1)S(1)}, u32[]{:S(2)}, u32[]{:S(2)}) %all-to-all-start.1) | async-done | bytes 852000 | tf_op jit(solution)/shard_map/all_to_all | solution.py:281
  69.9 1.0 %shard_map.91 = (bf16[208,1024]{1,0:T(8,128)(2,1)}, bf16[208,1024]{1,0:T(8,128)(2,1)}) custom-call(bf16[8,2,208,128]{3,2,1,0:T(8,128)(2,1)S(1)} %all-to-all-done.1.in_ref), custom_call_target="tpu_custom_call" | custom-call | bytes 1703936 | tf_op jit(solution)/shard_map/pallas_call | solution.py:194
Async XLA Ops:
  0.6 14.4 %copy-start.2 = (bf16[128,512]{1,0:T(8,128)(2,1)S(1)}, bf16[128,512]{1,0:T(8,128)(2,1)}, u32[]{:S(2)}) copy-start(bf16[128,512]{1,0:T(8,128)(2,1)} %param.6) | copy-start | bytes 393220
  0.6 22.4 %copy-start.3 = (bf16[128,512]{1,0:T(8,128)(2,1)S(1)}, bf16[128,512]{1,0:T(8,128)(2,1)}, u32[]{:S(2)}) copy-start(bf16[128,512]{1,0:T(8,128)(2,1)} %param.9) | copy-start | bytes 393220
  0.7 29.7 %copy-start.1 = (s32[64]{0:T(128)S(1)}, s32[64]{0:T(128)}, u32[]{:S(2)}) copy-start(s32[64]{0:T(128)} %text_ref.1) | copy-start | bytes 772
  0.7 29.7 %copy-start = (s32[64]{0:T(128)S(1)}, s32[64]{0:T(128)}, u32[]{:S(2)}) copy-start(s32[64]{0:T(128)} %counts_ref.1) | copy-start | bytes 772
  2.8 31.7 %all-to-all-start = ((bf16[8,2,208,128]{3,2,1,0:T(8,128)(2,1)}), bf16[8,2,208,128]{3,2,1,0:T(8,128)(2,1)S(1)}, u32[]{:S(2)}, u32[]{:S(2)}) async-start(bf16[8,2,208,128]{3,2,1,0:T(8,128)(2,1)} %shard_map.86), calls=%async_computation | async-start | bytes 1703936 | tf_op jit(solution)/shard_map/all_to_all | solution.py:242
  44.6 25.3 %all-to-all-start.1 = ((bf16[8,2,208,128]{3,2,1,0:T(8,128)(2,1)}), bf16[8,2,208,128]{3,2,1,0:T(8,128)(2,1)S(1)}, u32[]{:S(2)}, u32[]{:S(2)}) async-start(bf16[8,2,208,128]{3,2,1,0:T(8,128)(2,1)} %get-tuple-element.24), calls=%async_computation.1 | async-start | bytes 1703936 | tf_op jit(solution)/shard_map/all_to_all | solution.py:281
